TPU v7x, 256 devices: a whole 4x4x8 slice. The times are simulated.
256 devices in a mesh: row: 128 (over z_lo, x, y, core), col: 2 (over z_hi).
Axes of the slice: x: 4, y: 4, z: 8 (z_hi: 2, z_lo: 4; z = z_hi * 4 + z_lo), core: 2. Of those that a mesh axis runs over, the one named last changes fastest.
Arguments:
- snapshot: float32 [4, 262144, 512], P(None, 'row', 'col'), may hold values from -6 to 6
- range_test: float32 [4, 129, 512], P(None, None, 'col'), may hold values from -0.125 to 0.125
- corange_test: float32 [129, 262144], P(None, 'row'), may hold values from -0.01171875 to 0.01171875
- core_left: float32 [259, 262144], P(None, 'row'), may hold values from -0.01171875 to 0.01171875
- core_right: float32 [4, 259, 512], P(None, None, 'col'), may hold values from -0.125 to 0.125
- range_sketch: float32 [129, 262144], P(None, ('row', 'col')), may hold values from -6 to 6
- core_sketch: float32 [259, 259], replicated, may hold values from -6 to 6
Outputs:
- range_out: float32 [129, 262144], P(None, ('row', 'col'))
- corange_out: float32 [4, 129, 512], P(None, None, 'col')
- core_out: float32 [259, 259], replicated
All inputs are finite; a program needn't handle non-finite values.
Results may differ from a plain program's by a relative error of at most 0.0001.
Values sent between devices are 32-bit elements; how exact they have to be, the bound alone decides.
No kernel may reach another device: no remote copies, remote signals or barrier semaphores. Data moves between devices by JAX's collectives and lax.ppermute only.
A program may use at most 64 MiB of HBM per device.

v0:
```python
import jax
import jax.numpy as jnp
from jax import lax
from jax.sharding import PartitionSpec as P


def on_device(snapshot, range_test, corange_test, core_left, core_right, range_sketch, core_sketch):
    highest = lax.Precision.HIGHEST
    partial_value = jnp.einsum(
        "jkc,jrc->kr", range_test, snapshot, precision=highest, preferred_element_type=jnp.float32
    )
    summed = lax.psum(partial_value, "col")
    half_width = range_sketch.shape[1]
    summed = lax.dynamic_slice_in_dim(summed, lax.axis_index("col") * half_width, half_width, 1)
    range_out = range_sketch + summed
    corange_part = jnp.einsum(
        "kr,jrc->jkc", corange_test, snapshot, precision=highest, preferred_element_type=jnp.float32
    )
    left_part = jnp.einsum(
        "sr,jrc->jsc", core_left, snapshot, precision=highest, preferred_element_type=jnp.float32
    )
    core_part = jnp.einsum(
        "jsc,jtc->st", left_part, core_right, precision=highest, preferred_element_type=jnp.float32
    )
    corange_out = lax.psum(corange_part, "row")
    core_total = lax.psum(core_part, ("row", "col"))
    core_out = core_sketch + core_total
    return (range_out, corange_out, core_out)


def solution(mesh):
    placed = (
        P(None, "row", "col"),
        P(None, None, "col"),
        P(None, "row"),
        P(None, "row"),
        P(None, None, "col"),
        P(None, ("row", "col")),
        P(),
    )
    return jax.shard_map(
        on_device,
        mesh=mesh,
        in_specs=placed,
        out_specs=(P(None, ("row", "col")), P(None, None, "col"), P()),
        check_vma=False,
    )
```

profile of v0, /device:TPU:1, one launch (start us, length us, event | category | flops | bytes accessed | tf_op | source)
XLA Modules:
  0.0 1583.9 jit_solution(15403366035185786427)
XLA Ops:
  7.2 0.0 copy-start
  7.2 0.0 all-reduce.8.cloned.1.call-start
  7.2 1.6 copy-done
  8.8 0.0 copy-start.2
  8.8 10.1 fusion.2
  18.9 0.0 copy-done.2
  18.9 0.0 copy-start.1
  18.9 2.7 convolution_bitcast_fusion.2
  21.6 0.0 all-reduce.8.cloned.1.call-update
  21.6 0.0 all-reduce.6.cloned.1.call-start
  21.7 0.0 copy-done.1
  21.7 8.0 convolution_bitcast_fusion.1
  29.7 0.0 all-reduce.6.cloned.1.call-update
  29.7 0.2 all-reduce.4.cloned.1.call-start
  29.9 13.2 convolution_bitcast_fusion
  43.1 0.0 copy-start.4
  43.1 0.0 all-reduce.4.cloned.1.call-update
  43.1 0.0 copy-start.3
  43.2 230.3 %all-reduce.8.cloned.1.call-done = f32[259,259]{1,0:T(8,128)} async-done(((f32[259,259]{1,0:T(8,128)}), f32[259,259]{1,0:T(8,128)}) %all-reduce.8.cloned.1.call-update) | async-done | bytes 268340 | tf_op jit(solution)/shard_map/psum | solution.py:26
  273.5 0.0 copy-done.4
  273.5 1.8 add.17
  275.2 1217.4 %all-reduce.6.cloned.1.call-done = f32[4,129,256]{2,1,0:T(8,128)} async-done(((f32[4,129,256]{2,1,0:T(8,128)}), f32[4,129,256]{2,1,0:T(8,128)}) %all-reduce.6.cloned.1.call-update) | async-done | bytes 528400 | tf_op jit(solution)/shard_map/psum | solution.py:25
  1492.6 2.1 copy.12
  1494.7 80.8 %all-reduce.4.cloned.1.call-done = f32[129,2048]{1,0:T(8,128)} async-done(((f32[129,2048]{1,0:T(8,128)}), f32[129,2048]{1,0:T(8,128)}) %all-reduce.4.cloned.1.call-update) | async-done | bytes 1056784 | tf_op jit(solution)/shard_map/psum | solution.py:12
  1575.5 0.0 copy-done.3
  1575.5 1.9 dynamic-slice_add_fusion
Async XLA Ops:
  7.2 1.6 copy-start
  7.2 266.3 %all-reduce.8.cloned.1.call-start = ((), (), s32[]{:S(2)}) async-start(), calls=%async_computation.2 | async-start | bytes 811008 | tf_op jit(solution)/shard_map/psum | solution.py:26
  8.8 10.1 copy-start.2
  18.9 2.8 copy-start.1
  21.6 1471.0 %all-reduce.6.cloned.1.call-start = ((), (), s32[]{:S(2)}) async-start(), calls=%async_computation.1 | async-start | bytes 1114112 | tf_op jit(solution)/shard_map/psum | solution.py:25
  29.7 1545.8 %all-reduce.4.cloned.1.call-start = ((), (), s32[]{:S(2)}) async-start(), calls=%async_computation | async-start | bytes 2228224 | tf_op jit(solution)/shard_map/psum | solution.py:12
  43.1 230.3 %copy-start.4 = (f32[259,259]{1,0:T(8,128)S(1)}, f32[259,259]{1,0:T(8,128)}, u32[]{:S(2)}) copy-start(f32[259,259]{1,0:T(8,128)} %param.13) | copy-start | bytes 804976
  43.1 1532.3 %copy-start.3 = (f32[129,1024]{1,0:T(8,128)S(1)}, f32[129,1024]{1,0:T(8,128)}, u32[]{:S(2)}) copy-start(f32[129,1024]{1,0:T(8,128)} %param.12) | copy-start | bytes 1585156
Sparse Core Ops, SparseCore 0:
  21.8 251.6 all-reduce.7
  276.6 1215.9 all-reduce.5
  1495.4 79.9 all-reduce.3
where the time goes:
time: 1580 us
  waiting for transfers between devices  1530 us (97%)
  matrix products  34 us (2%)
    psum x1, waiting for transfers between devices, on_device(): corange_out = lax.psum(corange_part, 'row')  1220 us
    psum x1, waiting for transfers between devices, on_device(): core_total = lax.psum(core_part, ('row', 'col'))  230 us
    psum x1, waiting for transfers between devices, on_device(): summed = lax.psum(partial_value, 'col')  80.8 us
  transfers between devices with their start and end apart: 3, of which 3 were waited for; matrix products, arithmetic and copies ran while one was open for 2% of the time, Pallas kernels for 0%

commit v1 on v0

v1 whole, which is shorter than its diff:
```python
import jax
import jax.numpy as jnp
from jax import lax
from jax.experimental import pallas as pl
from jax.experimental.pallas import tpu as pltpu
from jax.sharding import Mesh
from jax.sharding import PartitionSpec as P

ROWS = 896
CORE_AT = 544
EXTRA_AT = 808
CHUNK = 56
BLOCK = 256


def split(x):
    high = x.astype(jnp.bfloat16)
    low = (x - high.astype(jnp.float32)).astype(jnp.bfloat16)
    return high, low


def products(
    place, snap_ref, range_test_ref, corange_ref, left_ref, right_ref, sketch_ref,
    send_ref, keep_ref, mine_ref, other_ref,
    test_cat, corange_acc, left_acc,
):
    step = pl.program_id(0)
    steps = pl.num_programs(0)
    slabs, _, cols = snap_ref.shape

    @pl.when(step == 0)
    def _():
        for j in range(slabs):
            high, low = split(range_test_ref[j])
            at = 3 * cols * j
            test_cat[:, at : at + cols] = high
            test_cat[:, at + cols : at + 2 * cols] = high
            test_cat[:, at + 2 * cols : at + 3 * cols] = low
        corange_acc[...] = jnp.zeros_like(corange_acc)
        left_acc[...] = jnp.zeros_like(left_acc)

    high, low = split(corange_ref[...])
    corange_cat = jnp.concatenate([high, high, low], axis=1)
    high, low = split(left_ref[...])
    left_cat = jnp.concatenate([high, high, low], axis=1)
    pieces = []
    for j in range(slabs):
        high, low = split(snap_ref[j])
        pieces += [high, low, high]
        snap_cat = jnp.concatenate([high, low, high], axis=0)
        corange_acc[j] += jnp.dot(corange_cat, snap_cat, preferred_element_type=jnp.float32)
        left_acc[j] += jnp.dot(left_cat, snap_cat, preferred_element_type=jnp.float32)
    range_part = lax.dot_general(
        test_cat[...], jnp.concatenate(pieces, axis=1), (((1,), (1,)), ((), ())),
        preferred_element_type=jnp.float32,
    )

    @pl.when(step < steps // 2)
    def _():
        send_ref[...] = range_part

    @pl.when(step >= steps // 2)
    def _():
        keep_ref[...] = sketch_ref[...] + range_part

    @pl.when(step == steps - 1)
    def _():
        size = right_ref.shape[1]
        lefts, rights = [], []
        for j in range(slabs):
            high, low = split(left_acc[j])
            lefts += [high, high, low]
            high, low = split(right_ref[j])
            rights += [high, low, high]
        left_all = jnp.concatenate(lefts, axis=1)
        right_all = jnp.concatenate(rights, axis=1)
        core = lax.dot_general(
            left_all, right_all[:256], (((1,), (1,)), ((), ())), preferred_element_type=jnp.float32
        )
        extra = lax.dot_general(
            right_all[256:], left_all, (((1,), (1,)), ((), ())), preferred_element_type=jnp.float32
        )
        more = size - 256
        for own in range(2):

            @pl.when(place[1] == own)
            def _():
                for half, out in ((own, mine_ref), (1 - own, other_ref)):
                    lanes = slice(128 * half, 128 * half + 128)
                    out[...] = jnp.zeros_like(out)
                    for j in range(slabs):
                        out[136 * j : 136 * j + corange_ref.shape[0], :] = corange_acc[j, :, lanes]
                    out[CORE_AT : CORE_AT + size, :] = core[:, lanes]
                    out[EXTRA_AT : EXTRA_AT + more, :] = extra[:, lanes]
                    if half == 0:
                        out[EXTRA_AT + 8 : EXTRA_AT + 8 + more, :more] = extra[:, 256:]


def finish(place, mine_ref, other_ref, core_sketch_ref, keep_ref, got_ref, range_ref, corange_ref, core_ref):
    range_ref[...] = keep_ref[...] + got_ref[...]
    slabs, rank, _ = corange_ref.shape
    size = core_ref.shape[0]
    more = size - 256
    for own in range(2):

        @pl.when(place[1] == own)
        def _():
            for half, part in ((own, mine_ref), (1 - own, other_ref)):
                lanes = slice(128 * half, 128 * half + 128)
                for j in range(slabs):
                    corange_ref[j, :, lanes] = part[136 * j : 136 * j + rank, :]
                core_ref[:, lanes] = core_sketch_ref[:, lanes] + part[CORE_AT : CORE_AT + size, :]
                block = jnp.concatenate([part[EXTRA_AT : EXTRA_AT + 8, :], jnp.zeros((120, 128), jnp.float32)], axis=0)
                turned = block.T
                core_ref[lanes, 256:] = core_sketch_ref[lanes, 256:] + turned[:, :more]
                if half == 0:
                    block = jnp.concatenate(
                        [part[EXTRA_AT + 8 : EXTRA_AT + 16, :], jnp.zeros((120, 128), jnp.float32)], axis=0
                    )
                    turned = block.T
                    core_ref[256:, 256:] = core_sketch_ref[256:, 256:] + turned[:more, :more]


def on_device(snapshot, range_test, corange_test, core_left, core_right, range_sketch, core_sketch):
    slabs, rows, cols = snapshot.shape
    rank = range_test.shape[1]
    size = core_left.shape[0]
    width = rows // 2
    steps = rows // BLOCK
    half = steps // 2
    column = lax.axis_index("zh")
    core = lax.axis_index("core")
    place = jnp.stack([column, core]).astype(jnp.int32)

    def turn(i, p):
        return lax.rem(i + half * (1 - p[0]), steps)

    vmem = pl.BlockSpec(memory_space=pltpu.VMEM)
    send, keep, mine, other = pl.pallas_call(
        products,
        out_shape=(
            jax.ShapeDtypeStruct((rank, width), jnp.float32),
            jax.ShapeDtypeStruct((rank, width), jnp.float32),
            jax.ShapeDtypeStruct((ROWS, 128), jnp.float32),
            jax.ShapeDtypeStruct((ROWS, 128), jnp.float32),
        ),
        grid_spec=pltpu.PrefetchScalarGridSpec(
            num_scalar_prefetch=1,
            grid=(steps,),
            in_specs=[
                pl.BlockSpec((slabs, BLOCK, cols), lambda i, p: (0, turn(i, p), 0)),
                pl.BlockSpec((slabs, rank, cols), lambda i, p: (0, 0, 0)),
                pl.BlockSpec((rank, BLOCK), lambda i, p: (0, turn(i, p))),
                pl.BlockSpec((size, BLOCK), lambda i, p: (0, turn(i, p))),
                pl.BlockSpec((slabs, size, cols), lambda i, p: (0, 0, 0)),
                pl.BlockSpec((rank, BLOCK), lambda i, p: (0, jnp.maximum(i - half, 0))),
            ],
            out_specs=[
                pl.BlockSpec((rank, BLOCK), lambda i, p: (0, jnp.minimum(i, half - 1))),
                pl.BlockSpec((rank, BLOCK), lambda i, p: (0, jnp.maximum(i - half, 0))),
                pl.BlockSpec((ROWS, 128), lambda i, p: (0, 0)),
                pl.BlockSpec((ROWS, 128), lambda i, p: (0, 0)),
            ],
            scratch_shapes=[
                pltpu.VMEM((rank, 3 * cols * slabs), jnp.bfloat16),
                pltpu.VMEM((slabs, rank, cols), jnp.float32),
                pltpu.VMEM((slabs, size, cols), jnp.float32),
            ],
        ),
        compiler_params=pltpu.CompilerParams(vmem_limit_bytes=40 * 2**20),
        cost_estimate=pl.CostEstimate(flops=7_000_000_000, bytes_accessed=15_000_000, transcendentals=0),
        name="products",
    )(place, snapshot, range_test, corange_test, core_left, core_right, range_sketch)

    got = lax.ppermute(send, "zh", [(0, 1), (1, 0)])
    swap = [(0, 1), (1, 0)]
    part = mine + lax.ppermute(other, "core", swap)
    pieces = lax.all_to_all(part.reshape(16, CHUNK, 128), ("x", "y"), 0, 0, tiled=True)
    piece = pieces.sum(axis=0)
    stack = lax.all_to_all(jnp.broadcast_to(piece[None], (8, CHUNK, 128)), ("zh", "zl"), 0, 0, tiled=True)
    at = CHUNK * lax.axis_index(("x", "y")) + lax.broadcasted_iota(jnp.int32, (CHUNK, 128), 0)
    both = stack.reshape(2, 4, CHUNK, 128).sum(axis=1)
    total = jnp.where(at >= CORE_AT, both[0] + both[1], jnp.where(column == 0, both[0], both[1]))
    mine = lax.all_to_all(jnp.broadcast_to(total[None], (16, CHUNK, 128)), ("x", "y"), 0, 0, tiled=True)
    mine = mine.reshape(ROWS, 128)
    other = lax.ppermute(mine, "core", swap)

    return pl.pallas_call(
        finish,
        out_shape=(
            jax.ShapeDtypeStruct((rank, width), jnp.float32),
            jax.ShapeDtypeStruct((slabs, rank, cols), jnp.float32),
            jax.ShapeDtypeStruct((size, size), jnp.float32),
        ),
        in_specs=[pl.BlockSpec(memory_space=pltpu.SMEM)] + [vmem] * 5,
        out_specs=[vmem] * 3,
        compiler_params=pltpu.CompilerParams(vmem_limit_bytes=40 * 2**20),
        name="finish",
    )(place, mine, other, core_sketch, keep, got)


def solution(mesh):
    fine = Mesh(mesh.devices.reshape(4, 4, 4, 2, 2), ("zl", "x", "y", "core", "zh"))
    row = ("zl", "x", "y", "core")
    placed = (
        P(None, row, "zh"),
        P(None, None, "zh"),
        P(None, row),
        P(None, row),
        P(None, None, "zh"),
        P(None, row + ("zh",)),
        P(),
    )
    return jax.shard_map(
        on_device,
        mesh=fine,
        in_specs=placed,
        out_specs=(P(None, row + ("zh",)), P(None, None, "zh"), P()),
        check_vma=False,
    )
```

time: 1580 us -> 92.8 us (0.06)
  the two profiles are of different devices: /device:TPU:1 before, /device:TPU:6 now
where the time goes in v1:
time: 92.8 us; the launch traced here: 92.4 us
  waiting for transfers between devices  37.9 us (41%)
  blocking collectives  16.3 us (18%)
  Pallas kernels  15.8 us (17%)
  starting transfers between devices  14.9 us (16%)
  local copies, waits for them, and re-layouts  6.56 us (7%)
    ppermute x1, waiting for transfers between devices, on_device(): got = lax.ppermute(send, 'zh', [(0, 1), (1, 0)])  18.7 us
    all_to_all x1, blocking collectives, on_device(): lax.all_to_all(part.reshape(16, CHUNK, 128), ('x', 'y'), 0, 0, tiled=True)  16.3 us
    pallas_call x1, Pallas kernels, on_device(): pl.pallas_call(products, out_shape=(jax.ShapeDtypeStruct((rank, width), j...  14.1 us
    all_to_all x1, waiting for transfers between devices, on_device(): lax.all_to_all(jnp.broadcast_to(piece[None], (8, CHUNK, 128)), ('zh', 'zl...  10.1 us
    all_to_all x1, starting transfers between devices, on_device(): lax.all_to_all(jnp.broadcast_to(piece[None], (8, CHUNK, 128)), ('zh', 'zl...  8.6 us
    all_to_all x1, waiting for transfers between devices, on_device(): lax.all_to_all(jnp.broadcast_to(total[None], (16, CHUNK, 128)), ('x', 'y'...  7.19 us
    all_to_all x1, starting transfers between devices, on_device(): lax.all_to_all(jnp.broadcast_to(total[None], (16, CHUNK, 128)), ('x', 'y'...  5.67 us
    unnamed x10, local copies, waits for them, and re-layouts  4.06 us
  transfers between devices with their start and end apart: 5, of which 4 were waited for; matrix products, arithmetic and copies ran while one was open for 0% of the time, Pallas kernels for 0%

profile of v1, /device:TPU:6, one launch (start us, length us, event | category | flops | bytes accessed | tf_op | source)
XLA Modules:
  0.0 92.4 jit_solution(16165140937758290471)
XLA Ops:
  0.6 0.0 copy-start.1
  0.6 1.3 %copy.13.range_test_ref = f32[4,129,256]{2,1,0:T(8,128)S(1)} copy(f32[4,129,256]{2,0,1:T(4,128)} %param.8) | data formatting | bytes 1056768 | tf_op args[1]
  1.9 0.0 copy-start.3
  2.0 1.5 %copy.14.right_ref = f32[4,259,256]{2,1,0:T(8,128)S(1)} copy(f32[4,259,256]{2,0,1:T(4,128)} %param.11) | data formatting | bytes 2121728 | tf_op args[4]
  3.5 0.1 pad_add_fusion.place
  3.5 0.0 copy-done.1
  3.5 0.0 copy-done.3
  3.5 0.0 copy-start.2
  3.5 1.2 %copy-done.2 = f32[129,2048]{1,0:T(8,128)S(1)} copy-done((f32[129,2048]{1,0:T(8,128)S(1)}, f32[129,2048]{1,0:T(8,128)}, u32[]{:S(2)}) %copy-start.2) | copy-done | bytes 1056792
  4.8 14.1 %products.1 = (f32[129,1024]{1,0:T(8,128)S(1)}, f32[129,1024]{1,0:T(8,128)S(1)}, f32[896,128]{1,0:T(8,128)S(1)}, f32[896,128]{1,0:T(8,128)S(1)}) custom-call(s32[2]{0:T(128)S(1)} %pad_add_fusion.place, f32[4,2048,256]{2,1,0:T(8,128)} %snap_ref.1, f32[4,129,256]{2,1,0:T(8,128)S(1)} %copy.13.range_test_ref, f32[129,2048]{1,0:T(8,128)S(1)} %copy-done.2, ...), custom_call_target="tpu_custom_call" | custom-call | flops 7000000000 | bytes 15000000 | tf_op jit(solution)/shard_map/products/pallas_call | solution.py:139
  18.9 0.1 collective-permute-start
  19.0 1.8 %collective-permute-done = f32[896,128]{1,0:T(8,128)S(1)} collective-permute-done((f32[896,128]{1,0:T(8,128)S(1)}, f32[896,128]{1,0:T(8,128)S(1)}, u32[]{:S(2)}, u32[]{:S(2)}) %collective-permute-start) | collective-permute-done | bytes 458784 | tf_op jit(solution)/shard_map/ppermute | solution.py:177
  20.9 16.3 %all_to_all.15 = f32[16,56,128]{2,1,0:T(8,128)S(1)} all-to-all(f32[16,56,128]{2,1,0:T(8,128)S(1)} %bitcast.10), channel_id=1, replica_groups=mesh['zl'=4,'x'=4,'y'=4,'core'=2,'zh'=2] {'x','y'}, dimensions={0} | all-to-all | bytes 917504 | tf_op jit(solution)/shard_map/all_to_all | solution.py:178
  37.2 0.7 broadcast_in_dim.6
  37.9 0.0 copy-start
  37.9 8.6 %all-to-all-start.1 = ((f32[8,56,128]{2,1,0:T(8,128)}), f32[8,56,128]{2,1,0:T(8,128)S(1)}, u32[]{:S(2)}, u32[]{:S(2)}) async-start(f32[8,56,128]{2,1,0:T(8,128)} %broadcast_in_dim.6), calls=%async_computation.1 | async-start | bytes 458752 | tf_op jit(solution)/shard_map/all_to_all | solution.py:180
  46.5 10.1 %all-to-all-done.1 = f32[8,56,128]{2,1,0:T(8,128)S(1)} async-done(((f32[8,56,128]{2,1,0:T(8,128)}), f32[8,56,128]{2,1,0:T(8,128)S(1)}, u32[]{:S(2)}, u32[]{:S(2)}) %all-to-all-start.1) | async-done | bytes 229408 | tf_op jit(solution)/shard_map/all_to_all | solution.py:180
  56.7 0.1 select_bitcast_fusion
  56.8 0.8 broadcast_in_dim.16
  57.6 5.7 %all-to-all-start.2 = ((f32[16,56,128]{2,1,0:T(8,128)}), f32[16,56,128]{2,1,0:T(8,128)S(1)}, u32[]{:S(2)}, u32[]{:S(2)}) async-start(f32[16,56,128]{2,1,0:T(8,128)} %broadcast_in_dim.16), calls=%async_computation.2 | async-start | bytes 917504 | tf_op jit(solution)/shard_map/all_to_all | solution.py:184
  63.2 0.6 collective-permute-start.2
  63.8 7.2 %all-to-all-done.2 = f32[16,56,128]{2,1,0:T(8,128)S(1)} async-done(((f32[16,56,128]{2,1,0:T(8,128)}), f32[16,56,128]{2,1,0:T(8,128)S(1)}, u32[]{:S(2)}, u32[]{:S(2)}) %all-to-all-start.2) | async-done | bytes 458784 | tf_op jit(solution)/shard_map/all_to_all | solution.py:184
  71.0 0.0 collective-permute-start.1
  71.0 18.7 %collective-permute-done.2.got_ref = f32[129,1024]{1,0:T(8,128)S(1)} collective-permute-done((f32[129,1024]{1,0:T(8,128)S(1)}, f32[129,1024]{1,0:T(8,128)S(1)}, u32[]{:S(2)}, u32[]{:S(2)}) %collective-permute-start.2) | collective-permute-done | bytes 528416 | tf_op jit(solution)/shard_map/ppermute | solution.py:175
  89.7 0.0 collective-permute-done.1.other_ref
  89.7 0.0 copy-done
  89.7 1.7 %finish.1 = (f32[129,1024]{1,0:T(8,128)}, f32[4,129,256]{2,1,0:T(8,128)S(1)}, f32[259,259]{1,0:T(8,128)}) custom-call(s32[2]{0:T(128)S(1)} %pad_add_fusion.place, f32[896,128]{1,0:T(8,128)S(1)} %bitcast.9, f32[896,128]{1,0:T(8,128)S(1)} %collective-permute-done.1.other_ref, f32[259,259]{1,0:T(8,128)S(1)} %copy-done, ...), custom_call_target="tpu_custom_call" | custom-call | tf_op jit(solution)/shard_map/finish/pallas_call | solution.py:188
  91.4 1.0 %copy.15 = f32[4,129,256]{2,0,1:T(4,128)} copy(f32[4,129,256]{2,1,0:T(8,128)S(1)} %get-tuple-element.15) | data formatting | bytes 1056768 | tf_op jit(solution)/shard_map/finish/pallas_call | solution.py:188
  (4 shorter events, 0.1 us)
Async XLA Ops:
  0.6 2.9 %copy-start.1 = (f32[259,2048]{1,0:T(8,128)S(1)}, f32[259,2048]{1,0:T(8,128)}, u32[]{:S(2)}) copy-start(f32[259,2048]{1,0:T(8,128)} %left_ref.1) | copy-start | bytes 6365188
  1.9 1.6 %copy-start.3 = (f32[129,1024]{1,0:T(8,128)S(1)}, f32[129,1024]{1,0:T(8,128)}, u32[]{:S(2)}) copy-start(f32[129,1024]{1,0:T(8,128)} %sketch_ref.1) | copy-start | bytes 1585156
  3.5 1.2 %copy-start.2 = (f32[129,2048]{1,0:T(8,128)S(1)}, f32[129,2048]{1,0:T(8,128)}, u32[]{:S(2)}) copy-start(f32[129,2048]{1,0:T(8,128)} %corange_ref.1) | copy-start | bytes 3170308
  18.9 1.9 %collective-permute-start = (f32[896,128]{1,0:T(8,128)S(1)}, f32[896,128]{1,0:T(8,128)S(1)}, u32[]{:S(2)}, u32[]{:S(2)}) collective-permute-start(f32[896,128]{1,0:T(8,128)S(1)} %get-tuple-element.8), channel_id=1, source_target_pairs={{0,2},{2,0},{1,3},{3,1},{4,6},{6,4},{5,7},{7,5},{8,10},{10,8},{9,1... | collective-permute-start | bytes 1376264 | tf_op jit(solution)/shard_map/ppermute | solution.py:177
  37.9 51.8 %copy-start = (f32[259,259]{1,0:T(8,128)S(1)}, f32[259,259]{1,0:T(8,128)}, u32[]{:S(2)}) copy-start(f32[259,259]{1,0:T(8,128)} %core_sketch_ref.1) | copy-start | bytes 804976
  37.9 18.7 %all-to-all-start.1 = ((f32[8,56,128]{2,1,0:T(8,128)}), f32[8,56,128]{2,1,0:T(8,128)S(1)}, u32[]{:S(2)}, u32[]{:S(2)}) async-start(f32[8,56,128]{2,1,0:T(8,128)} %broadcast_in_dim.6), calls=%async_computation.1 | async-start | bytes 458752 | tf_op jit(solution)/shard_map/all_to_all | solution.py:180
  57.6 13.4 %all-to-all-start.2 = ((f32[16,56,128]{2,1,0:T(8,128)}), f32[16,56,128]{2,1,0:T(8,128)S(1)}, u32[]{:S(2)}, u32[]{:S(2)}) async-start(f32[16,56,128]{2,1,0:T(8,128)} %broadcast_in_dim.16), calls=%async_computation.2 | async-start | bytes 917504 | tf_op jit(solution)/shard_map/all_to_all | solution.py:184
  63.2 26.5 %collective-permute-start.2 = (f32[129,1024]{1,0:T(8,128)S(1)}, f32[129,1024]{1,0:T(8,128)S(1)}, u32[]{:S(2)}, u32[]{:S(2)}) collective-permute-start(f32[129,1024]{1,0:T(8,128)S(1)} %get-tuple-element.10), channel_id=1, source_target_pairs={{0,1},{1,0},{2,3},{3,2},{4,5},{5,4},{6,7},{7,6},{8,9},{9,8},{10,11... | collective-permute-start | bytes 1585160 | tf_op jit(solution)/shard_map/ppermute | solution.py:175
  71.0 18.8 %collective-permute-start.1 = (f32[896,128]{1,0:T(8,128)S(1)}, f32[896,128]{1,0:T(8,128)S(1)}, u32[]{:S(2)}, u32[]{:S(2)}) collective-permute-start(f32[896,128]{1,0:T(8,128)S(1)} %bitcast.8), channel_id=1, source_target_pairs={{0,2},{2,0},{1,3},{3,1},{4,6},{6,4},{5,7},{7,5},{8,10},{10,8},{9,1... | collective-permute-start | bytes 1376264 | tf_op jit(solution)/shard_map/ppermute | solution.py:186

commit v2 on v0

v2 whole, which is shorter than its diff:
```python
import jax
import jax.numpy as jnp
from jax import lax
from jax.experimental import pallas as pl
from jax.experimental.pallas import tpu as pltpu
from jax.sharding import Mesh
from jax.sharding import PartitionSpec as P

ROWS = 896
CORE_AT = 544
EXTRA_AT = 808
CHUNK = 56
SLAB = 136
LEFT_AT = 144
PIECE = 512
SPANS = ((0, 1024),)


def split(x):
    high = x.astype(jnp.bfloat16)
    low = (x - high.astype(jnp.float32)).astype(jnp.bfloat16)
    return high, low


NT = (((1,), (1,)), ((), ()))


def reductions(place, snap_ref, corange_ref, left_ref, right_hbm, mine_ref, other_ref, tests, acc, pay, core_acc, extra_acc, right, sem):
    slab = pl.program_id(0)
    rank = corange_ref.shape[0]
    size = left_ref.shape[0]
    more = size - 256

    @pl.when(slab == 0)
    def _():
        for j in range(right.shape[0]):
            pltpu.make_async_copy(right_hbm.at[:, j, :], right.at[j], sem.at[j]).start()
        high, low = split(corange_ref[...])
        tests[:rank] = jnp.concatenate([high, high, low], axis=1)
        high, low = split(left_ref[...])
        tests[LEFT_AT:] = jnp.concatenate([high, high, low], axis=1)
        core_acc[...] = jnp.zeros_like(core_acc)
        extra_acc[...] = jnp.zeros_like(extra_acc)

    high, low = split(snap_ref[0])
    acc[...] = jnp.dot(tests[...], jnp.concatenate([high, low, high], axis=0), preferred_element_type=jnp.float32)
    for half in range(2):
        pay[place[1] ^ half, pl.ds(pl.multiple_of(SLAB * slab, 8), SLAB), :] = acc[:SLAB, 128 * half : 128 * half + 128]
    high, low = split(acc[LEFT_AT:])
    left = jnp.concatenate([high, high, low], axis=1)
    pltpu.make_async_copy(right_hbm.at[:, 0, :], right.at[slab], sem.at[slab]).wait()
    high, low = split(right[slab])
    turned = jnp.concatenate([high, low, high], axis=1)
    core_acc[:size] += lax.dot_general(left, turned[:256], NT, preferred_element_type=jnp.float32)
    extra_acc[:more] += lax.dot_general(turned[256:], left, NT, preferred_element_type=jnp.float32)

    @pl.when(slab == pl.num_programs(0) - 1)
    def _():
        for half in range(2):
            lanes = slice(128 * half, 128 * half + 128)
            own = place[1] ^ half
            pay[own, CORE_AT : CORE_AT + size, :] = core_acc[:size, lanes]
            pay[own, EXTRA_AT : EXTRA_AT + 8, :] = extra_acc[:, lanes]
        pay[place[1], EXTRA_AT + 8 : EXTRA_AT + 16, :more] = extra_acc[:, 256:]
        mine_ref[...] = pay[0]
        other_ref[...] = pay[1]


def range_half(place, snap_hbm, test_hbm, *rest):
    *extra, out_ref, snap, test, test_sem, sem = rest
    kept = extra[0] if len(extra) and extra[0].shape[0] == out_ref.shape[0] and len(extra) == 2 else None
    slabs, width, _ = snap.shape
    count = width // PIECE
    at = place[0] * width
    loads = [pltpu.make_async_copy(test_hbm.at[:, j, :], test.at[j], test_sem.at[j]) for j in range(slabs)]
    for copy in loads:
        copy.start()
    copies = []
    for c in range(count):
        copy = pltpu.make_async_copy(
            snap_hbm.at[:, pl.ds(pl.multiple_of(at + c * PIECE, PIECE), PIECE), :],
            snap.at[:, pl.ds(c * PIECE, PIECE), :],
            sem.at[c],
        )
        copy.start()
        copies.append(copy)
    tests = []
    for j in range(slabs):
        loads[j].wait()
        high, low = split(test[j])
        tests += [high, high, low]
    tests = jnp.concatenate(tests, axis=1)
    for c in range(count):
        copies[c].wait()
        pieces = []
        for j in range(slabs):
            high, low = split(snap[j, c * PIECE : (c + 1) * PIECE, :])
            pieces += [high, low, high]
        cols = slice(c * PIECE, (c + 1) * PIECE)
        part = lax.dot_general(tests, jnp.concatenate(pieces, axis=1), NT, preferred_element_type=jnp.float32)
        out_ref[:, cols] = part if kept is None else kept[:, cols] + part


def add_two(a_ref, b_ref, *rest):
    rest[-1][...] = a_ref[...] + b_ref[...]


def sum_pieces(pieces_ref, *rest):
    out_ref = rest[-1]
    total = pieces_ref[0]
    for k in range(1, pieces_ref.shape[0]):
        total += pieces_ref[k]
    for k in range(out_ref.shape[0]):
        out_ref[k] = total


def sum_stack(place, stack_ref, *rest):
    out_ref = rest[-1]
    near = stack_ref[4 * place[0]]
    far = stack_ref[4 - 4 * place[0]]
    for k in range(1, 4):
        near += stack_ref[4 * place[0] + k]
        far += stack_ref[4 - 4 * place[0] + k]
    at = CHUNK * place[2] + lax.broadcasted_iota(jnp.int32, near.shape, 0)
    total = jnp.where(at >= CORE_AT, near + far, near)
    for k in range(out_ref.shape[0]):
        out_ref[k] = total


def finish(place, mine_ref, other_ref, core_sketch_ref, keep_ref, *rest):
    *got_refs, range_ref, corange_ref, core_ref = rest
    at = 0
    for got in got_refs:
        cols = slice(at, at + got.shape[1])
        range_ref[:, cols] = keep_ref[:, cols] + got[...]
        at += got.shape[1]
    rank, slabs, _ = corange_ref.shape
    size = core_ref.shape[0]
    more = size - 256
    for own in range(2):

        @pl.when(place[1] == own)
        def _():
            for half, part in ((own, mine_ref), (1 - own, other_ref)):
                lanes = slice(128 * half, 128 * half + 128)
                for j in range(slabs):
                    corange_ref[:, j, lanes] = part[SLAB * j : SLAB * j + rank, :]
                core_ref[:, lanes] = core_sketch_ref[:, lanes] + part[CORE_AT : CORE_AT + size, :]
                block = jnp.concatenate([part[EXTRA_AT : EXTRA_AT + 8, :], jnp.zeros((120, 128), jnp.float32)], axis=0)
                turned = block.T
                core_ref[lanes, 256:] = core_sketch_ref[lanes, 256:] + turned[:, :more]
                if half == 0:
                    block = jnp.concatenate(
                        [part[EXTRA_AT + 8 : EXTRA_AT + 16, :], jnp.zeros((120, 128), jnp.float32)], axis=0
                    )
                    turned = block.T
                    core_ref[256:, 256:] = core_sketch_ref[256:, 256:] + turned[:more, :more]


def on_device(snapshot, range_test, corange_test, core_left, core_right, range_sketch, core_sketch):
    slabs, rows, cols = snapshot.shape
    rank = range_test.shape[1]
    size = core_left.shape[0]
    width = rows // 2
    column = lax.axis_index("zh")
    place = jnp.stack([column, lax.axis_index("core"), lax.axis_index(("x", "y"))]).astype(jnp.int32)
    flip = jnp.stack([1 - column]).astype(jnp.int32)
    vmem = pl.BlockSpec(memory_space=pltpu.VMEM)
    smem = pl.BlockSpec(memory_space=pltpu.SMEM)
    anywhere = pl.BlockSpec(memory_space=pl.ANY)
    params = pltpu.CompilerParams(vmem_limit_bytes=16 * 2**20)
    f32 = lambda *shape: jax.ShapeDtypeStruct(shape, jnp.float32)

    def cost(us):
        return pl.CostEstimate(flops=int(us * 1e9), bytes_accessed=int(us * 3e6), transcendentals=0)

    mine, other = pl.pallas_call(
        reductions,
        out_shape=(f32(ROWS, 128), f32(ROWS, 128)),
        grid_spec=pltpu.PrefetchScalarGridSpec(
            num_scalar_prefetch=1,
            grid=(slabs,),
            in_specs=[
                pl.BlockSpec((1, rows, cols), lambda i, p: (i, 0, 0)),
                pl.BlockSpec((rank, rows), lambda i, p: (0, 0)),
                pl.BlockSpec((size, rows), lambda i, p: (0, 0)),
                anywhere,
            ],
            out_specs=[pl.BlockSpec((ROWS, 128), lambda i, p: (0, 0))] * 2,
            scratch_shapes=[
                pltpu.VMEM((LEFT_AT + size, 3 * rows), jnp.bfloat16),
                pltpu.VMEM((LEFT_AT + size, cols), jnp.float32),
                pltpu.VMEM((2, ROWS, 128), jnp.float32),
                pltpu.VMEM((264, 256), jnp.float32),
                pltpu.VMEM((8, size), jnp.float32),
                pltpu.VMEM((slabs, size, cols), jnp.float32),
                pltpu.SemaphoreType.DMA((slabs,)),
            ],
        ),
        compiler_params=pltpu.CompilerParams(vmem_limit_bytes=60 * 2**20),
        cost_estimate=cost(9),
        name="reductions",
    )(place, snapshot, corange_test, core_left, jnp.transpose(core_right, (1, 0, 2)))

    def range_part(name, where, kept, *more):
        return pl.pallas_call(
            range_half,
            out_shape=f32(rank, width),
            in_specs=[smem, anywhere, anywhere] + [vmem] * kept + [anywhere] * (len(more) - kept),
            out_specs=vmem,
            scratch_shapes=[
                pltpu.VMEM((slabs, width, cols), jnp.float32),
                pltpu.VMEM((slabs, rank, cols), jnp.float32),
                pltpu.SemaphoreType.DMA((slabs,)),
                pltpu.SemaphoreType.DMA((width // PIECE,)),
            ],
            compiler_params=pltpu.CompilerParams(vmem_limit_bytes=54 * 2**20),
            cost_estimate=cost(5),
            name=name,
        )(where, snapshot, jnp.transpose(range_test, (1, 0, 2)), *more)

    def add_up(kernel, name, shape, *args):
        specs = [smem] * (kernel is sum_stack) + [vmem] * (1 + (kernel is add_two))
        specs += [anywhere] * (len(args) - len(specs))
        return pl.pallas_call(
            kernel,
            out_shape=f32(*shape),
            in_specs=specs,
            out_specs=vmem,
            compiler_params=params,
            cost_estimate=cost(1),
            name=name,
        )(*args)

    swap = [(0, 1), (1, 0)]
    send = range_part("range_send", flip, 0, mine)
    part = add_up(add_two, "add_two", (ROWS, 128), mine, lax.ppermute(other, "core", swap), send)
    got = [lax.ppermute(send[:, a:b], "zh", swap) for a, b in SPANS] if len(SPANS) > 1 else [lax.ppermute(send, "zh", swap)]

    def reduce(part):
        pieces = lax.all_to_all(part.reshape(16, CHUNK, 128), ("x", "y"), 0, 0, tiled=True)
        keep = range_part("range_keep", place, 1, range_sketch, part)
        copies = add_up(sum_pieces, "sum_pieces", (8, CHUNK, 128), pieces, keep)
        stack = lax.all_to_all(copies, ("zh", "zl"), 0, 0, tiled=True)
        copies = add_up(sum_stack, "sum_stack", (16, CHUNK, 128), place, stack)
        mine = lax.all_to_all(copies, ("x", "y"), 0, 0, tiled=True).reshape(ROWS, 128)
        return mine, keep

    def nothing(part):
        return jnp.zeros((ROWS, 128), jnp.float32), jnp.zeros((rank, width), jnp.float32)

    mine, keep = lax.cond(place[0] >= 0, reduce, nothing, part)
    other = lax.ppermute(mine, "core", swap)

    range_out, corange_out, core_out = pl.pallas_call(
        finish,
        out_shape=(f32(rank, width), f32(rank, slabs, cols), f32(size, size)),
        in_specs=[smem] + [vmem] * (4 + len(got)),
        out_specs=[vmem] * 3,
        compiler_params=params,
        cost_estimate=cost(2),
        name="finish",
    )(place, mine, other, core_sketch, keep, *got)
    return range_out, jnp.transpose(corange_out, (1, 0, 2)), core_out


def solution(mesh):
    fine = Mesh(mesh.devices.reshape(4, 4, 4, 2, 2), ("zl", "x", "y", "core", "zh"))
    row = ("zl", "x", "y", "core")
    placed = (
        P(None, row, "zh"),
        P(None, None, "zh"),
        P(None, row),
        P(None, row),
        P(None, None, "zh"),
        P(None, row + ("zh",)),
        P(),
    )
    return jax.shard_map(
        on_device,
        mesh=fine,
        in_specs=placed,
        out_specs=(P(None, row + ("zh",)), P(None, None, "zh"), P()),
        check_vma=False,
    )
```

time: 1580 us -> 85.7 us (0.05)
  waiting for transfers between devices: 1530 us -> 5.56 us
  matrix products: 34 us -> 0 us
  blocking collectives: 0 us -> 31.8 us
  Pallas kernels: 0 us -> 28.7 us
  starting transfers between devices: 0.3 us -> 17.4 us
    psum x3 -> x0, waiting for transfers between devices: 1530 us -> none  [the longest x1 1220 us: on_device(): corange_out = lax.psum(corange_part, 'row')]
    dot_general x4 -> x0, matrix products: 34 us -> none  [the longest x1 13.2 us: on_device(): jnp.einsum('jkc,jrc->kr', range_test, snapshot, precision=highest, prefer...]
    all_to_all x0 -> x2, blocking collectives: none -> 31.8 us  [the longest x1 17.3 us: reduce(): lax.all_to_all(copies, ('x', 'y'), 0, 0, tiled=True).reshape(ROWS, 128)]
    pallas_call x0 -> x7, Pallas kernels: none -> 28.7 us  [the longest x1 13.8 us: on_device(): pl.pallas_call(reductions, out_shape=(f32(ROWS, 128), f32(ROWS, 128)), gr...]
  transfers between devices with their start and end apart: 3 -> 4, of which waited for: 3 -> 2; matrix products, arithmetic and copies ran while one was open for 2% -> 0% of each run, Pallas kernels for 0% -> 14%
where the time goes in v2:
time: 85.7 us; the launch traced here: 85.4 us
  blocking collectives  31.8 us (37%)
  Pallas kernels  28.7 us (33%)
  starting transfers between devices  17.4 us (20%)
  waiting for transfers between devices  5.56 us (6%)
  local copies, waits for them, and re-layouts  1.1 us (1%)
    all_to_all x1, blocking collectives, reduce(): lax.all_to_all(copies, ('x', 'y'), 0, 0, tiled=True).reshape(ROWS, 128)  17.3 us
    all_to_all x1, blocking collectives, reduce(): stack = lax.all_to_all(copies, ('zh', 'zl'), 0, 0, tiled=True)  14.5 us
    pallas_call x1, Pallas kernels, on_device(): pl.pallas_call(reductions, out_shape=(f32(ROWS, 128), f32(ROWS, 128)), gr...  13.8 us
    pallas_call x2, Pallas kernels, range_part(): pl.pallas_call(range_half, out_shape=f32(rank, width), in_specs=[smem, an...  10.9 us
    all_to_all x1, starting transfers between devices, reduce(): lax.all_to_all(part.reshape(16, CHUNK, 128), ('x', 'y'), 0, 0, tiled=True)  6.88 us
    ppermute x1, starting transfers between devices, on_device(): lax.ppermute(send, 'zh', swap)  5.26 us
    all_to_all x1, waiting for transfers between devices, reduce(): lax.all_to_all(part.reshape(16, CHUNK, 128), ('x', 'y'), 0, 0, tiled=True)  4.11 us
    ppermute x1, starting transfers between devices, on_device(): lax.ppermute(other, 'core', swap)  3.33 us
  transfers between devices with their start and end apart: 4, of which 2 were waited for; matrix products, arithmetic and copies ran while one was open for 0% of the time, Pallas kernels for 14%

profile of v2, /device:TPU:1, one launch (start us, length us, event | category | flops | bytes accessed | tf_op | source)
XLA Modules:
  0.0 85.4 jit_solution(6047838339628126522)
XLA Ops:
  0.6 0.1 pad_add_fusion.place
  0.7 0.0 copy-start.4
  0.7 13.8 %reductions.1 = (f32[896,128]{1,0:T(8,128)}, f32[896,128]{1,0:T(8,128)}) custom-call(s32[3]{0:T(128)S(1)} %pad_add_fusion.place, f32[4,2048,256]{2,1,0:T(8,128)} %snap_hbm.1, f32[129,2048]{1,0:T(8,128)} %corange_ref.1, f32[259,2048]{1,0:T(8,128)} %left_ref.1, f32[259,4,256]{2,1,0:T(4,128)} %bitcast.11), custom_call_target="tpu_custom_call" | custom-call | flops 8999999488 | bytes 27000000 | tf_op jit(solution)/shard_map/reductions/pallas_call | solution.py:177
  14.5 3.3 %collective-permute-start = (f32[896,128]{1,0:T(8,128)}, f32[896,128]{1,0:T(8,128)S(1)}, u32[]{:S(2)}, u32[]{:S(2)}) collective-permute-start(f32[896,128]{1,0:T(8,128)} %get-tuple-element.26), channel_id=1, source_target_pairs={{0,2},{2,0},{1,3},{3,1},{4,6},{6,4},{5,7},{7,5},{8,10},{10,8},{9,1... | collective-permute-start | bytes 1376264 | tf_op jit(solution)/shard_map/ppermute | solution.py:237
  17.8 0.0 copy-done.4
  17.8 0.0 copy-start.2
  17.8 0.0 copy-start.3
  17.8 5.2 %range_send.1.rest_0_ = f32[129,1024]{1,0:T(8,128)} custom-call(s32[1]{0:T(128)} %bitcast.7.place, f32[4,2048,256]{2,1,0:T(8,128)} %snap_hbm.1, f32[129,4,256]{2,1,0:T(4,128)S(1)} %bitcast.12, f32[896,128]{1,0:T(8,128)} %get-tuple-element.25.rest_0_.a_ref), custom_call_target="tpu_custom_call" | custom-call | flops 5000000000 | bytes 15000000 | tf_op jit(solution)/shard_map/range_send/pallas_call | solution.py:206
  23.0 5.3 %collective-permute-start.2 = (f32[129,1024]{1,0:T(8,128)}, f32[129,1024]{1,0:T(8,128)S(1)}, u32[]{:S(2)}, u32[]{:S(2)}) collective-permute-start(f32[129,1024]{1,0:T(8,128)} %range_send.1.rest_0_), channel_id=1, source_target_pairs={{0,1},{1,0},{2,3},{3,2},{4,5},{5,4},{6,7},{7,6},{8,9},{9,8},{10,11... | collective-permute-start | bytes 1585160 | tf_op jit(solution)/shard_map/ppermute | solution.py:238
  28.3 0.0 collective-permute-done.b_ref
  28.3 0.0 copy-done.2
  28.3 0.0 copy-start
  28.3 1.1 %copy-done = f32[129,1024]{1,0:T(8,128)S(1)} copy-done((f32[129,1024]{1,0:T(8,128)S(1)}, f32[129,1024]{1,0:T(8,128)}, u32[]{:S(2)}) %copy-start) | copy-done | bytes 528408
  29.4 0.8 add_two.1
  30.2 0.0 copy-done.3
  30.2 0.0 copy-start.1
  30.2 49.2 %conditional.1 = (f32[896,128]{1,0:T(8,128)S(1)}, f32[129,1024]{1,0:T(8,128)}) conditional(s32[]{:T(128)} %convert_element_type.3, () %tuple.16, (f32[896,128]{1,0:T(8,128)}, f32[4,129,256]{2,0,1:T(4,128)S(1)}, s32[3]{0:T(128)S(1)}, f32[4,2048,256]{2,1,0:T(8,128)}, f32[129,1024]{1,0:T(8,128)S(1)}) %tuple.22), branch_computations={%region_0.0_spmd, %region_1.0_spmd} | conditional | flops 7000000000 | bytes 23752560 | solution.py:252
  30.2 6.9 %all-to-all-start = ((f32[16,56,128]{2,1,0:T(8,128)}), f32[16,56,128]{2,1,0:T(8,128)S(1)}, u32[]{:S(2)}, u32[]{:S(2)}) async-start(f32[16,56,128]{2,1,0:T(8,128)} %bitcast), calls=%async_computation | async-start | bytes 917504 | tf_op jit(solution)/shard_map/cond/branch_1_fun/all_to_all | solution.py:241
  37.1 5.7 %range_keep.1.rest_0_ = f32[129,1024]{1,0:T(8,128)} custom-call(s32[3]{0:T(128)S(1)} %get-tuple-element.10.place, f32[4,2048,256]{2,1,0:T(8,128)} %get-tuple-element.12.snap_hbm, f32[129,4,256]{2,1,0:T(4,128)S(1)} %bitcast.13, f32[129,1024]{1,0:T(8,128)S(1)} %get-tuple-element.33.rest_0_, f32[896,128]{1,0:T(8,128)} %get-tuple-element.11.rest_1_), custom_call_target="tpu_custom_call" | custom-call | flops 5000000000 | bytes 15000000 | tf_op jit(solution)/shard_map/cond/branch_1_fun/range_keep/pallas_call | solution.py:206
  42.8 4.1 %all-to-all-done.pieces_ref = f32[16,56,128]{2,1,0:T(8,128)S(1)} async-done(((f32[16,56,128]{2,1,0:T(8,128)}), f32[16,56,128]{2,1,0:T(8,128)S(1)}, u32[]{:S(2)}, u32[]{:S(2)}) %all-to-all-start) | async-done | bytes 458784 | tf_op jit(solution)/shard_map/cond/branch_1_fun/all_to_all | solution.py:241
  47.0 14.5 %all_to_all.12.stack_ref = f32[8,56,128]{2,1,0:T(8,128)S(1)} all-to-all(f32[8,56,128]{2,1,0:T(8,128)S(1)} %sum_pieces.1), channel_id=1, replica_groups=mesh['zl'=4,'x'=4,'y'=4,'core'=2,'zh'=2] {'zh','zl'}, dimensions={0} | all-to-all | bytes 458752 | tf_op jit(solution)/shard_map/cond/branch_1_fun/all_to_all | solution.py:244
  61.4 0.6 sum_stack.1
  62.0 17.3 %all_to_all.13 = f32[16,56,128]{2,1,0:T(8,128)S(1)} all-to-all(f32[16,56,128]{2,1,0:T(8,128)S(1)} %sum_stack.1), channel_id=1, replica_groups=mesh['zl'=4,'x'=4,'y'=4,'core'=2,'zh'=2] {'x','y'}, dimensions={0} | all-to-all | bytes 917504 | tf_op jit(solution)/shard_map/cond/branch_1_fun/all_to_all | solution.py:246
  79.3 2.0 %collective-permute-start.1 = (f32[896,128]{1,0:T(8,128)S(1)}, f32[896,128]{1,0:T(8,128)S(1)}, u32[]{:S(2)}, u32[]{:S(2)}) collective-permute-start(f32[896,128]{1,0:T(8,128)S(1)} %get-tuple-element.27.mine_ref), channel_id=1, source_target_pairs={{0,2},{2,0},{1,3},{3,1},{4,6},{6,4},{5,7},{7,5},{8,10},{10,8},{9,1... | collective-permute-start | bytes 1376264 | tf_op jit(solution)/shard_map/ppermute | solution.py:253
  81.3 0.0 collective-permute-done.2.rest_0_
  81.3 1.4 %collective-permute-done.1.other_ref = f32[896,128]{1,0:T(8,128)S(1)} collective-permute-done((f32[896,128]{1,0:T(8,128)S(1)}, f32[896,128]{1,0:T(8,128)S(1)}, u32[]{:S(2)}, u32[]{:S(2)}) %collective-permute-start.1) | collective-permute-done | bytes 458784 | tf_op jit(solution)/shard_map/ppermute | solution.py:253
  82.8 0.0 copy-done.1
  82.8 2.6 %finish.1 = (f32[129,1024]{1,0:T(8,128)}, f32[129,4,256]{2,1,0:T(4,128)}, f32[259,259]{1,0:T(8,128)}) custom-call(s32[3]{0:T(128)S(1)} %pad_add_fusion.place, f32[896,128]{1,0:T(8,128)S(1)} %get-tuple-element.27.mine_ref, f32[896,128]{1,0:T(8,128)S(1)} %collective-permute-done.1.other_ref, f32[259,259]{1,0:T(8,128)S(1)} %copy-done.1, ...), custom_call_target="tpu_custom_call" | custom-call | flops 2000000000 | bytes 6000000 | tf_op jit(solution)/shard_map/finish/pallas_call | solution.py:255
  (1 shorter events, 0.0 us)
Async XLA Ops:
  0.7 17.1 %copy-start.4 = (f32[4,129,256]{2,0,1:T(4,128)S(1)}, f32[4,129,256]{2,0,1:T(4,128)}, u32[]{:S(2)}) copy-start(f32[4,129,256]{2,0,1:T(4,128)} %param.10) | copy-start | bytes 1585156
  14.5 13.8 %collective-permute-start = (f32[896,128]{1,0:T(8,128)}, f32[896,128]{1,0:T(8,128)S(1)}, u32[]{:S(2)}, u32[]{:S(2)}) collective-permute-start(f32[896,128]{1,0:T(8,128)} %get-tuple-element.26), channel_id=1, source_target_pairs={{0,2},{2,0},{1,3},{3,1},{4,6},{6,4},{5,7},{7,5},{8,10},{10,8},{9,1... | collective-permute-start | bytes 1376264 | tf_op jit(solution)/shard_map/ppermute | solution.py:237
  17.8 10.4 %copy-start.2 = (f32[896,128]{1,0:T(8,128)S(1)}, f32[896,128]{1,0:T(8,128)}, u32[]{:S(2)}) copy-start(f32[896,128]{1,0:T(8,128)} %get-tuple-element.25.rest_0_.a_ref) | copy-start | bytes 1376260
  17.8 12.3 %copy-start.3 = (f32[129,1024]{1,0:T(8,128)S(1)}, f32[129,1024]{1,0:T(8,128)}, u32[]{:S(2)}) copy-start(f32[129,1024]{1,0:T(8,128)} %param.14) | copy-start | bytes 1585156
  23.0 58.3 %collective-permute-start.2 = (f32[129,1024]{1,0:T(8,128)}, f32[129,1024]{1,0:T(8,128)S(1)}, u32[]{:S(2)}, u32[]{:S(2)}) collective-permute-start(f32[129,1024]{1,0:T(8,128)} %range_send.1.rest_0_), channel_id=1, source_target_pairs={{0,1},{1,0},{2,3},{3,2},{4,5},{5,4},{6,7},{7,6},{8,9},{9,8},{10,11... | collective-permute-start | bytes 1585160 | tf_op jit(solution)/shard_map/ppermute | solution.py:238
  28.3 1.1 %copy-start = (f32[129,1024]{1,0:T(8,128)S(1)}, f32[129,1024]{1,0:T(8,128)}, u32[]{:S(2)}) copy-start(f32[129,1024]{1,0:T(8,128)} %range_send.1.rest_0_) | copy-start | bytes 1585156
  30.2 52.6 %copy-start.1 = (f32[259,259]{1,0:T(8,128)S(1)}, f32[259,259]{1,0:T(8,128)}, u32[]{:S(2)}) copy-start(f32[259,259]{1,0:T(8,128)} %core_sketch_ref.1) | copy-start | bytes 804976
  30.2 16.7 %all-to-all-start = ((f32[16,56,128]{2,1,0:T(8,128)}), f32[16,56,128]{2,1,0:T(8,128)S(1)}, u32[]{:S(2)}, u32[]{:S(2)}) async-start(f32[16,56,128]{2,1,0:T(8,128)} %bitcast), calls=%async_computation | async-start | bytes 917504 | tf_op jit(solution)/shard_map/cond/branch_1_fun/all_to_all | solution.py:241
  79.3 3.4 %collective-permute-start.1 = (f32[896,128]{1,0:T(8,128)S(1)}, f32[896,128]{1,0:T(8,128)S(1)}, u32[]{:S(2)}, u32[]{:S(2)}) collective-permute-start(f32[896,128]{1,0:T(8,128)S(1)} %get-tuple-element.27.mine_ref), channel_id=1, source_target_pairs={{0,2},{2,0},{1,3},{3,1},{4,6},{6,4},{5,7},{7,5},{8,10},{10,8},{9,1... | collective-permute-start | bytes 1376264 | tf_op jit(solution)/shard_map/ppermute | solution.py:253

commit v3 on v2

--- a/solution.py
+++ b/solution.py
@@ -13,7 +13,7 @@
 SLAB = 136
 LEFT_AT = 144
 PIECE = 512
-SPANS = ((0, 1024),)
+BLOCK = 512
 
 
 def split(x):
@@ -25,43 +25,57 @@
 NT = (((1,), (1,)), ((), ()))
 
 
-def reductions(place, snap_ref, corange_ref, left_ref, right_hbm, mine_ref, other_ref, tests, acc, pay, core_acc, extra_acc, right, sem):
-    slab = pl.program_id(0)
+def products(
+    place, snap_ref, corange_ref, left_ref, right_hbm, after,
+    mine_ref, other_ref,
+    tests, acc, pay, core_acc, extra_acc, right, sem,
+):
+    step = pl.program_id(0)
+    steps = pl.num_programs(0)
+    slabs, _, cols = snap_ref.shape
     rank = corange_ref.shape[0]
     size = left_ref.shape[0]
     more = size - 256
-
-    @pl.when(slab == 0)
+    loads = [pltpu.make_async_copy(right_hbm.at[:, j, :], right.at[j], sem.at[j]) for j in range(slabs)]
+
+    @pl.when(step == 0)
     def _():
-        for j in range(right.shape[0]):
-            pltpu.make_async_copy(right_hbm.at[:, j, :], right.at[j], sem.at[j]).start()
-        high, low = split(corange_ref[...])
-        tests[:rank] = jnp.concatenate([high, high, low], axis=1)
-        high, low = split(left_ref[...])
-        tests[LEFT_AT:] = jnp.concatenate([high, high, low], axis=1)
-        core_acc[...] = jnp.zeros_like(core_acc)
-        extra_acc[...] = jnp.zeros_like(extra_acc)
-
-    high, low = split(snap_ref[0])
-    acc[...] = jnp.dot(tests[...], jnp.concatenate([high, low, high], axis=0), preferred_element_type=jnp.float32)
-    for half in range(2):
-        pay[place[1] ^ half, pl.ds(pl.multiple_of(SLAB * slab, 8), SLAB), :] = acc[:SLAB, 128 * half : 128 * half + 128]
-    high, low = split(acc[LEFT_AT:])
-    left = jnp.concatenate([high, high, low], axis=1)
-    pltpu.make_async_copy(right_hbm.at[:, 0, :], right.at[slab], sem.at[slab]).wait()
-    high, low = split(right[slab])
-    turned = jnp.concatenate([high, low, high], axis=1)
-    core_acc[:size] += lax.dot_general(left, turned[:256], NT, preferred_element_type=jnp.float32)
-    extra_acc[:more] += lax.dot_general(turned[256:], left, NT, preferred_element_type=jnp.float32)
-
-    @pl.when(slab == pl.num_programs(0) - 1)
+        for copy in loads:
+            copy.start()
+        acc[...] = jnp.zeros_like(acc)
+        tests[rank:LEFT_AT] = jnp.zeros((LEFT_AT - rank, tests.shape[1]), jnp.bfloat16)
+
+    high, low = split(corange_ref[...])
+    tests[:rank] = jnp.concatenate([high, high, low], axis=1)
+    high, low = split(left_ref[...])
+    tests[LEFT_AT:] = jnp.concatenate([high, high, low], axis=1)
+    for j in range(slabs):
+        high, low = split(snap_ref[j])
+        acc[j] += jnp.dot(
+            tests[...], jnp.concatenate([high, low, high], axis=0), preferred_element_type=jnp.float32
+        )
+
+    @pl.when(step == steps - 1)
     def _():
+        lefts, rights = [], []
+        for j in range(slabs):
+            for half in range(2):
+                pay[place[1] ^ half, SLAB * j : SLAB * (j + 1), :] = acc[j, :SLAB, 128 * half : 128 * half + 128]
+            loads[j].wait()
+            high, low = split(acc[j, LEFT_AT:])
+            lefts += [high, high, low]
+            high, low = split(right[j])
+            rights += [high, low, high]
+        left_all = jnp.concatenate(lefts, axis=1)
+        right_all = jnp.concatenate(rights, axis=1)
+        core_acc[:size] = lax.dot_general(left_all, right_all[:256], NT, preferred_element_type=jnp.float32)
+        extra_acc[:more] = lax.dot_general(right_all[256:], left_all, NT, preferred_element_type=jnp.float32)
         for half in range(2):
             lanes = slice(128 * half, 128 * half + 128)
             own = place[1] ^ half
             pay[own, CORE_AT : CORE_AT + size, :] = core_acc[:size, lanes]
-            pay[own, EXTRA_AT : EXTRA_AT + 8, :] = extra_acc[:, lanes]
-        pay[place[1], EXTRA_AT + 8 : EXTRA_AT + 16, :more] = extra_acc[:, 256:]
+            pay[own, EXTRA_AT : EXTRA_AT + more, :] = extra_acc[:more, lanes]
+        pay[place[1], EXTRA_AT + 8 : EXTRA_AT + 8 + more, :more] = extra_acc[:more, 256:]
         mine_ref[...] = pay[0]
         other_ref[...] = pay[1]
 
@@ -101,10 +115,6 @@
         out_ref[:, cols] = part if kept is None else kept[:, cols] + part
 
 
-def add_two(a_ref, b_ref, *rest):
-    rest[-1][...] = a_ref[...] + b_ref[...]
-
-
 def sum_pieces(pieces_ref, *rest):
     out_ref = rest[-1]
     total = pieces_ref[0]
@@ -127,13 +137,7 @@
         out_ref[k] = total
 
 
-def finish(place, mine_ref, other_ref, core_sketch_ref, keep_ref, *rest):
-    *got_refs, range_ref, corange_ref, core_ref = rest
-    at = 0
-    for got in got_refs:
-        cols = slice(at, at + got.shape[1])
-        range_ref[:, cols] = keep_ref[:, cols] + got[...]
-        at += got.shape[1]
+def finish(place, mine_ref, other_ref, core_sketch_ref, corange_ref, core_ref):
     rank, slabs, _ = corange_ref.shape
     size = core_ref.shape[0]
     more = size - 256
@@ -174,34 +178,7 @@
     def cost(us):
         return pl.CostEstimate(flops=int(us * 1e9), bytes_accessed=int(us * 3e6), transcendentals=0)
 
-    mine, other = pl.pallas_call(
-        reductions,
-        out_shape=(f32(ROWS, 128), f32(ROWS, 128)),
-        grid_spec=pltpu.PrefetchScalarGridSpec(
-            num_scalar_prefetch=1,
-            grid=(slabs,),
-            in_specs=[
-                pl.BlockSpec((1, rows, cols), lambda i, p: (i, 0, 0)),
-                pl.BlockSpec((rank, rows), lambda i, p: (0, 0)),
-                pl.BlockSpec((size, rows), lambda i, p: (0, 0)),
-                anywhere,
-            ],
-            out_specs=[pl.BlockSpec((ROWS, 128), lambda i, p: (0, 0))] * 2,
-            scratch_shapes=[
-                pltpu.VMEM((LEFT_AT + size, 3 * rows), jnp.bfloat16),
-                pltpu.VMEM((LEFT_AT + size, cols), jnp.float32),
-                pltpu.VMEM((2, ROWS, 128), jnp.float32),
-                pltpu.VMEM((264, 256), jnp.float32),
-                pltpu.VMEM((8, size), jnp.float32),
-                pltpu.VMEM((slabs, size, cols), jnp.float32),
-                pltpu.SemaphoreType.DMA((slabs,)),
-            ],
-        ),
-        compiler_params=pltpu.CompilerParams(vmem_limit_bytes=60 * 2**20),
-        cost_estimate=cost(9),
-        name="reductions",
-    )(place, snapshot, corange_test, core_left, jnp.transpose(core_right, (1, 0, 2)))
-
+    tests_first = jnp.transpose(range_test, (1, 0, 2))
     def range_part(name, where, kept, *more):
         return pl.pallas_call(
             range_half,
@@ -217,10 +194,10 @@
             compiler_params=pltpu.CompilerParams(vmem_limit_bytes=54 * 2**20),
             cost_estimate=cost(5),
             name=name,
-        )(where, snapshot, jnp.transpose(range_test, (1, 0, 2)), *more)
+        )(where, snapshot, tests_first, *more)
 
     def add_up(kernel, name, shape, *args):
-        specs = [smem] * (kernel is sum_stack) + [vmem] * (1 + (kernel is add_two))
+        specs = [smem] * (kernel is sum_stack) + [vmem]
         specs += [anywhere] * (len(args) - len(specs))
         return pl.pallas_call(
             kernel,
@@ -232,35 +209,74 @@
             name=name,
         )(*args)
 
+    rights_first = jnp.transpose(core_right, (1, 0, 2))
     swap = [(0, 1), (1, 0)]
-    send = range_part("range_send", flip, 0, mine)
-    part = add_up(add_two, "add_two", (ROWS, 128), mine, lax.ppermute(other, "core", swap), send)
-    got = [lax.ppermute(send[:, a:b], "zh", swap) for a, b in SPANS] if len(SPANS) > 1 else [lax.ppermute(send, "zh", swap)]
-
-    def reduce(part):
+    send = range_part("range_send", flip, 0)
+    got = lax.ppermute(send, "zh", swap)
+
+    def reduce(place, snapshot, tests_first, range_sketch, corange_test, core_left, rights_first, send, core_sketch):
+        steps = rows // BLOCK
+
+        mine, other = pl.pallas_call(
+            products,
+            out_shape=(f32(ROWS, 128), f32(ROWS, 128)),
+            grid_spec=pltpu.PrefetchScalarGridSpec(
+                num_scalar_prefetch=1,
+                grid=(steps,),
+                in_specs=[
+                    pl.BlockSpec((slabs, BLOCK, cols), lambda i, p: (0, i, 0)),
+                    pl.BlockSpec((rank, BLOCK), lambda i, p: (0, i)),
+                    pl.BlockSpec((size, BLOCK), lambda i, p: (0, i)),
+                    anywhere,
+                    anywhere,
+                ],
+                out_specs=[
+                    pl.BlockSpec((ROWS, 128), lambda i, p: (0, 0)),
+                    pl.BlockSpec((ROWS, 128), lambda i, p: (0, 0)),
+                ],
+                scratch_shapes=[
+                    pltpu.VMEM((LEFT_AT + size, 3 * BLOCK), jnp.bfloat16),
+                    pltpu.VMEM((slabs, LEFT_AT + size, cols), jnp.float32),
+                    pltpu.VMEM((2, ROWS, 128), jnp.float32),
+                    pltpu.VMEM((264, 256), jnp.float32),
+                    pltpu.VMEM((8, size), jnp.float32),
+                    pltpu.VMEM((slabs, size, cols), jnp.float32),
+                    pltpu.SemaphoreType.DMA((slabs,)),
+                ],
+            ),
+            compiler_params=pltpu.CompilerParams(vmem_limit_bytes=60 * 2**20),
+            cost_estimate=cost(9),
+            name="products",
+        )(place, snapshot, corange_test, core_left, rights_first, send)
+
+        part = mine + lax.ppermute(other, "core", swap)
         pieces = lax.all_to_all(part.reshape(16, CHUNK, 128), ("x", "y"), 0, 0, tiled=True)
-        keep = range_part("range_keep", place, 1, range_sketch, part)
-        copies = add_up(sum_pieces, "sum_pieces", (8, CHUNK, 128), pieces, keep)
+        copies = add_up(sum_pieces, "sum_pieces", (8, CHUNK, 128), pieces)
         stack = lax.all_to_all(copies, ("zh", "zl"), 0, 0, tiled=True)
-        copies = add_up(sum_stack, "sum_stack", (16, CHUNK, 128), place, stack)
+        keep = range_part("range_keep", place, 1, range_sketch, copies)
+        copies = add_up(sum_stack, "sum_stack", (16, CHUNK, 128), place, stack, keep)
         mine = lax.all_to_all(copies, ("x", "y"), 0, 0, tiled=True).reshape(ROWS, 128)
-        return mine, keep
-
-    def nothing(part):
-        return jnp.zeros((ROWS, 128), jnp.float32), jnp.zeros((rank, width), jnp.float32)
-
-    mine, keep = lax.cond(place[0] >= 0, reduce, nothing, part)
-    other = lax.ppermute(mine, "core", swap)
-
-    range_out, corange_out, core_out = pl.pallas_call(
-        finish,
-        out_shape=(f32(rank, width), f32(rank, slabs, cols), f32(size, size)),
-        in_specs=[smem] + [vmem] * (4 + len(got)),
-        out_specs=[vmem] * 3,
-        compiler_params=params,
-        cost_estimate=cost(2),
-        name="finish",
-    )(place, mine, other, core_sketch, keep, *got)
+        other = lax.ppermute(mine, "core", swap)
+        corange_out, core_out = pl.pallas_call(
+            finish,
+            out_shape=(f32(rank, slabs, cols), f32(size, size)),
+            in_specs=[smem] + [vmem] * 3,
+            out_specs=[vmem] * 2,
+            compiler_params=params,
+            cost_estimate=cost(2),
+            name="finish",
+        )(place, mine, other, core_sketch)
+        return keep, corange_out, core_out
+
+    def nothing(*_):
+        return tuple(jnp.zeros(shape, jnp.float32) for shape in ((rank, width), (rank, slabs, cols), (size, size)))
+
+    keep, corange_out, core_out = lax.cond(
+        place[0] >= 0, reduce, nothing,
+        place, snapshot, tests_first, range_sketch, corange_test, core_left, rights_first, send, core_sketch,
+    )
+    range_out = keep + got
+
     return range_out, jnp.transpose(corange_out, (1, 0, 2)), core_out
 
 

time: 85.7 us -> 79.5 us (0.928)
  Pallas kernels: 28.7 us -> 24.2 us
  blocking collectives: 31.8 us -> 28.7 us
  other arithmetic: 0.08 us -> 2.03 us
  waiting for transfers between devices: 5.56 us -> 6.92 us
  local copies, waits for them, and re-layouts: 1.1 us -> 0.03 us
    all_to_all x1, blocking collectives: 17.3 us -> 12.3 us  [reduce(): lax.all_to_all(copies, ('x', 'y'), 0, 0, tiled=True).reshape(ROWS, 128)]
    pallas_call x2, Pallas kernels: 16.4 us -> 12.7 us  [the longest x1 10.9 us: reduce(): pl.pallas_call(products, out_shape=(f32(ROWS, 128), f32(ROWS, 128)), grid...]
    all_to_all x1, starting transfers between devices: 6.88 us -> 3.4 us  [reduce(): stack = lax.all_to_all(copies, ('zh', 'zl'), 0, 0, tiled=True)]
    ppermute x3, starting transfers between devices: 10.6 us -> 13.2 us  [the longest x1 7.83 us: on_device(): got = lax.ppermute(send, 'zh', swap)]
    add x0 -> x2, other arithmetic: none -> 1.96 us  [the longest x1 1.09 us: reduce(): part = mine + lax.ppermute(other, 'core', swap)]
    all_to_all x1, blocking collectives: 14.5 us -> 16.4 us  [reduce(): lax.all_to_all(part.reshape(16, CHUNK, 128), ('x', 'y'), 0, 0, tiled=True)]
    ppermute x3, waiting for transfers between devices: 1.45 us -> 3.1 us  [the longest x1 1.65 us: reduce(): part = mine + lax.ppermute(other, 'core', swap)]
    unnamed x10 -> x2, local copies, waits for them, and re-layouts: 1.1 us -> 0.01 us
  transfers between devices with their start and end apart: 4 -> 4, of which waited for: 2 -> 3; matrix products, arithmetic and copies ran while one was open for 0% -> 1% of each run, Pallas kernels for 14% -> 24%
where the time goes in v3:
time: 79.5 us; the launch traced here: 79.1 us
  blocking collectives  28.7 us (36%)
  Pallas kernels  24.2 us (30%)
  starting transfers between devices  16.6 us (21%)
  waiting for transfers between devices  6.92 us (9%)
  other arithmetic  2.03 us (3%)
    all_to_all x1, blocking collectives, reduce(): lax.all_to_all(part.reshape(16, CHUNK, 128), ('x', 'y'), 0, 0, tiled=True)  16.4 us
    all_to_all x1, blocking collectives, reduce(): lax.all_to_all(copies, ('x', 'y'), 0, 0, tiled=True).reshape(ROWS, 128)  12.3 us
    pallas_call x1, Pallas kernels, reduce(): pl.pallas_call(products, out_shape=(f32(ROWS, 128), f32(ROWS, 128)), grid...  10.9 us
    pallas_call x2, Pallas kernels, range_part(): pl.pallas_call(range_half, out_shape=f32(rank, width), in_specs=[smem, an...  10.2 us
    ppermute x1, starting transfers between devices, on_device(): got = lax.ppermute(send, 'zh', swap)  7.83 us
    ppermute x1, starting transfers between devices, reduce(): other = lax.ppermute(mine, 'core', swap)  4.32 us
    all_to_all x1, waiting for transfers between devices, reduce(): stack = lax.all_to_all(copies, ('zh', 'zl'), 0, 0, tiled=True)  3.82 us
    all_to_all x1, starting transfers between devices, reduce(): stack = lax.all_to_all(copies, ('zh', 'zl'), 0, 0, tiled=True)  3.4 us
  transfers between devices with their start and end apart: 4, of which 3 were waited for; matrix products, arithmetic and copies ran while one was open for 1% of the time, Pallas kernels for 24%

profile of v3, /device:TPU:1, one launch (start us, length us, event | category | flops | bytes accessed | tf_op | source)
XLA Modules:
  0.0 79.1 jit_solution(5961357169067021431)
XLA Ops:
  0.6 0.0 copy-start.2
  0.6 5.3 %range_send.1 = f32[129,1024]{1,0:T(8,128)} custom-call(s32[1]{0:T(128)} %bitcast.6.place, f32[4,2048,256]{2,1,0:T(8,128)} %snap_hbm.1, f32[129,4,256]{2,1,0:T(4,128)} %bitcast.14), custom_call_target="tpu_custom_call" | custom-call | flops 5000000000 | bytes 15000000 | tf_op jit(solution)/shard_map/range_send/pallas_call | solution.py:183
  5.9 7.8 %collective-permute-start.2 = (f32[129,1024]{1,0:T(8,128)}, f32[129,1024]{1,0:T(8,128)S(1)}, u32[]{:S(2)}, u32[]{:S(2)}) collective-permute-start(f32[129,1024]{1,0:T(8,128)} %range_send.1), channel_id=1, source_target_pairs={{0,1},{1,0},{2,3},{3,2},{4,5},{5,4},{6,7},{7,6},{8,9},{9,8},{10,11... | collective-permute-start | bytes 1585160 | tf_op jit(solution)/shard_map/ppermute | solution.py:215
  13.7 0.1 pad_add_fusion
  13.8 0.0 copy-done.2
  13.8 64.4 %conditional.1 = (f32[129,1024]{1,0:T(8,128)S(1)}, f32[129,4,256]{2,1,0:T(4,128)}, f32[259,259]{1,0:T(8,128)}) conditional(s32[]{:T(128)} %convert_element_type.3, () %tuple.16, (s32[3]{0:T(128)S(1)}, f32[4,2048,256]{2,1,0:T(8,128)}, f32[129,2048]{1,0:T(8,128)}, f32[259,2048]{1,0:T(8,128)S(1)}, f32[259,4,256]{2,1,0:T(4,128)}, ...), branch_computations={%region_0.0_spmd, %region_1.0_spmd} | conditional | flops 18000113664 | bytes 71097128 | solution.py:274
  13.8 10.9 %products.1 = (f32[896,128]{1,0:T(8,128)}, f32[896,128]{1,0:T(8,128)}) custom-call(s32[3]{0:T(128)S(1)} %get-tuple-element.18.place, f32[4,2048,256]{2,1,0:T(8,128)} %get-tuple-element.19.snap_ref.snap_hbm, f32[129,2048]{1,0:T(8,128)} %get-tuple-element.44.corange_ref, f32[259,2048]{1,0:T(8,128)S(1)} %get-tuple-element.45.left_ref, ...), custom_call_target="tpu_custom_call" | custom-call | flops 8999999488 | bytes 27000000 | tf_op jit(solution)/shard_map/cond/branch_1_fun/products/pallas_call | solution.py:220
  24.7 1.0 %collective-permute-start = (f32[896,128]{1,0:T(8,128)}, f32[896,128]{1,0:T(8,128)S(1)}, u32[]{:S(2)}, u32[]{:S(2)}) collective-permute-start(f32[896,128]{1,0:T(8,128)} %get-tuple-element.27), channel_id=1, source_target_pairs={{0,2},{2,0},{1,3},{3,1},{4,6},{6,4},{5,7},{7,5},{8,10},{10,8},{9,1... | collective-permute-start | bytes 1376264 | tf_op jit(solution)/shard_map/cond/branch_1_fun/ppermute | solution.py:252
  25.7 1.7 %collective-permute-done = f32[896,128]{1,0:T(8,128)S(1)} collective-permute-done((f32[896,128]{1,0:T(8,128)}, f32[896,128]{1,0:T(8,128)S(1)}, u32[]{:S(2)}, u32[]{:S(2)}) %collective-permute-start) | collective-permute-done | bytes 458784 | tf_op jit(solution)/shard_map/cond/branch_1_fun/ppermute | solution.py:252
  27.4 1.1 %add.6 = f32[896,128]{1,0:T(8,128)S(1)} add(f32[896,128]{1,0:T(8,128)} %get-tuple-element.26, f32[896,128]{1,0:T(8,128)S(1)} %collective-permute-done) | non-fusion elementwise | flops 114688 | bytes 1376256 | tf_op jit(solution)/shard_map/cond/branch_1_fun/add | solution.py:252
  28.5 16.4 %all_to_all.12.pieces_ref = f32[16,56,128]{2,1,0:T(8,128)S(1)} all-to-all(f32[16,56,128]{2,1,0:T(8,128)S(1)} %bitcast.11), channel_id=1, replica_groups=mesh['zl'=4,'x'=4,'y'=4,'core'=2,'zh'=2] {'x','y'}, dimensions={0} | all-to-all | bytes 917504 | tf_op jit(solution)/shard_map/cond/branch_1_fun/all_to_all | solution.py:253
  44.8 0.0 copy-start.3
  44.8 0.0 copy-start.4
  44.8 0.7 sum_pieces.1.rest_1_
  45.6 3.4 %all-to-all-start.1 = ((f32[8,56,128]{2,1,0:T(8,128)}), f32[8,56,128]{2,1,0:T(8,128)S(1)}, u32[]{:S(2)}, u32[]{:S(2)}) async-start(f32[8,56,128]{2,1,0:T(8,128)} %sum_pieces.1.rest_1_), calls=%async_computation.1 | async-start | bytes 458752 | tf_op jit(solution)/shard_map/cond/branch_1_fun/all_to_all | solution.py:255
  49.0 0.0 copy-done.3
  49.0 0.0 copy-done.4
  49.0 4.9 %range_keep.1.rest_0_ = f32[129,1024]{1,0:T(8,128)S(1)} custom-call(s32[3]{0:T(128)S(1)} %get-tuple-element.18.place, f32[4,2048,256]{2,1,0:T(8,128)} %get-tuple-element.19.snap_ref.snap_hbm, f32[129,4,256]{2,1,0:T(4,128)S(1)} %copy-done.4, f32[129,1024]{1,0:T(8,128)S(1)} %copy-done.3, f32[8,56,128]{2,1,0:T(8,128)} %sum_pieces.1.rest_1_), custom_call_target="tpu_custom_call" | custom-call | flops 5000000000 | bytes 15000000 | tf_op jit(solution)/shard_map/cond/branch_1_fun/range_keep/pallas_call | solution.py:183
  53.9 0.0 copy-start
  54.0 0.0 copy-start.5
  54.0 3.8 %all-to-all-done.1.stack_ref = f32[8,56,128]{2,1,0:T(8,128)S(1)} async-done(((f32[8,56,128]{2,1,0:T(8,128)}), f32[8,56,128]{2,1,0:T(8,128)S(1)}, u32[]{:S(2)}, u32[]{:S(2)}) %all-to-all-start.1) | async-done | bytes 229408 | tf_op jit(solution)/shard_map/cond/branch_1_fun/all_to_all | solution.py:255
  57.8 0.6 sum_stack.1
  58.4 12.3 %all_to_all.13 = f32[16,56,128]{2,1,0:T(8,128)S(1)} all-to-all(f32[16,56,128]{2,1,0:T(8,128)S(1)} %sum_stack.1), channel_id=1, replica_groups=mesh['zl'=4,'x'=4,'y'=4,'core'=2,'zh'=2] {'x','y'}, dimensions={0} | all-to-all | bytes 917504 | tf_op jit(solution)/shard_map/cond/branch_1_fun/all_to_all | solution.py:258
  70.7 0.0 copy-done
  70.7 4.3 %collective-permute-start.1 = (f32[896,128]{1,0:T(8,128)S(1)}, f32[896,128]{1,0:T(8,128)S(1)}, u32[]{:S(2)}, u32[]{:S(2)}) collective-permute-start(f32[896,128]{1,0:T(8,128)S(1)} %bitcast.9), channel_id=1, source_target_pairs={{0,2},{2,0},{1,3},{3,1},{4,6},{6,4},{5,7},{7,5},{8,10},{10,8},{9,1... | collective-permute-start | bytes 1376264 | tf_op jit(solution)/shard_map/cond/branch_1_fun/ppermute | solution.py:259
  75.0 1.4 %collective-permute-done.1.other_ref = f32[896,128]{1,0:T(8,128)S(1)} collective-permute-done((f32[896,128]{1,0:T(8,128)S(1)}, f32[896,128]{1,0:T(8,128)S(1)}, u32[]{:S(2)}, u32[]{:S(2)}) %collective-permute-start.1) | collective-permute-done | bytes 458784 | tf_op jit(solution)/shard_map/cond/branch_1_fun/ppermute | solution.py:259
  76.4 0.0 copy-done.5
  76.4 0.0 copy-start.1
  76.4 1.8 %finish.1 = (f32[129,4,256]{2,1,0:T(4,128)}, f32[259,259]{1,0:T(8,128)}) custom-call(s32[3]{0:T(128)S(1)} %get-tuple-element.18.place, f32[896,128]{1,0:T(8,128)S(1)} %bitcast.10, f32[896,128]{1,0:T(8,128)S(1)} %collective-permute-done.1.other_ref, f32[259,259]{1,0:T(8,128)S(1)} %copy-done.5), custom_call_target="tpu_custom_call" | custom-call | flops 2000000000 | bytes 6000000 | tf_op jit(solution)/shard_map/cond/branch_1_fun/finish/pallas_call | solution.py:260
  78.3 0.0 copy-done.1
  78.3 0.0 collective-permute-done.2
  78.3 0.9 %add.10 = f32[129,1024]{1,0:T(8,128)} add(f32[129,1024]{1,0:T(8,128)S(1)} %get-tuple-element.37, f32[129,1024]{1,0:T(8,128)S(1)} %collective-permute-done.2) | non-fusion elementwise | flops 132096 | bytes 1585152 | tf_op jit(solution)/shard_map/add | solution.py:278
Async XLA Ops:
  0.6 13.2 %copy-start.2 = (f32[259,2048]{1,0:T(8,128)S(1)}, f32[259,2048]{1,0:T(8,128)}, u32[]{:S(2)}) copy-start(f32[259,2048]{1,0:T(8,128)} %param.12) | copy-start | bytes 6365188
  5.9 72.4 %collective-permute-start.2 = (f32[129,1024]{1,0:T(8,128)}, f32[129,1024]{1,0:T(8,128)S(1)}, u32[]{:S(2)}, u32[]{:S(2)}) collective-permute-start(f32[129,1024]{1,0:T(8,128)} %range_send.1), channel_id=1, source_target_pairs={{0,1},{1,0},{2,3},{3,2},{4,5},{5,4},{6,7},{7,6},{8,9},{9,8},{10,11... | collective-permute-start | bytes 1585160 | tf_op jit(solution)/shard_map/ppermute | solution.py:215
  24.7 2.7 %collective-permute-start = (f32[896,128]{1,0:T(8,128)}, f32[896,128]{1,0:T(8,128)S(1)}, u32[]{:S(2)}, u32[]{:S(2)}) collective-permute-start(f32[896,128]{1,0:T(8,128)} %get-tuple-element.27), channel_id=1, source_target_pairs={{0,2},{2,0},{1,3},{3,1},{4,6},{6,4},{5,7},{7,5},{8,10},{10,8},{9,1... | collective-permute-start | bytes 1376264 | tf_op jit(solution)/shard_map/cond/branch_1_fun/ppermute | solution.py:252
  44.8 4.1 %copy-start.3 = (f32[129,1024]{1,0:T(8,128)S(1)}, f32[129,1024]{1,0:T(8,128)}, u32[]{:S(2)}) copy-start(f32[129,1024]{1,0:T(8,128)} %get-tuple-element.46.rest_0_) | copy-start | bytes 1585156 | tf_op jit(solution)/shard_map/cond
  44.8 4.1 %copy-start.4 = (f32[129,4,256]{2,1,0:T(4,128)S(1)}, f32[129,4,256]{2,1,0:T(4,128)}, u32[]{:S(2)}) copy-start(f32[129,4,256]{2,1,0:T(4,128)} %get-tuple-element.20.test_hbm) | copy-start | bytes 1585156 | tf_op jit(solution)/shard_map/cond
  45.6 12.2 %all-to-all-start.1 = ((f32[8,56,128]{2,1,0:T(8,128)}), f32[8,56,128]{2,1,0:T(8,128)S(1)}, u32[]{:S(2)}, u32[]{:S(2)}) async-start(f32[8,56,128]{2,1,0:T(8,128)} %sum_pieces.1.rest_1_), calls=%async_computation.1 | async-start | bytes 458752 | tf_op jit(solution)/shard_map/cond/branch_1_fun/all_to_all | solution.py:255
  53.9 16.7 %copy-start = (f32[129,1024]{1,0:T(8,128)}, f32[129,1024]{1,0:T(8,128)S(1)}, u32[]{:S(2)}) copy-start(f32[129,1024]{1,0:T(8,128)S(1)} %range_keep.1.rest_0_) | copy-start | bytes 1585156 | tf_op jit(solution)/shard_map/cond
  54.0 22.5 %copy-start.5 = (f32[259,259]{1,0:T(8,128)S(1)}, f32[259,259]{1,0:T(8,128)}, u32[]{:S(2)}) copy-start(f32[259,259]{1,0:T(8,128)} %get-tuple-element.47.core_sketch_ref) | copy-start | bytes 804976 | tf_op jit(solution)/shard_map/cond
  70.7 5.8 %collective-permute-start.1 = (f32[896,128]{1,0:T(8,128)S(1)}, f32[896,128]{1,0:T(8,128)S(1)}, u32[]{:S(2)}, u32[]{:S(2)}) collective-permute-start(f32[896,128]{1,0:T(8,128)S(1)} %bitcast.9), channel_id=1, source_target_pairs={{0,2},{2,0},{1,3},{3,1},{4,6},{6,4},{5,7},{7,5},{8,10},{10,8},{9,1... | collective-permute-start | bytes 1376264 | tf_op jit(solution)/shard_map/cond/branch_1_fun/ppermute | solution.py:259
  76.4 1.8 %copy-start.1 = (f32[129,1024]{1,0:T(8,128)S(1)}, f32[129,1024]{1,0:T(8,128)}, u32[]{:S(2)}) copy-start(f32[129,1024]{1,0:T(8,128)} %copy-done) | copy-start | bytes 1585156 | tf_op jit(solution)/shard_map/cond

commit v4 on v3

--- a/solution.py
+++ b/solution.py
@@ -137,8 +137,14 @@
         out_ref[k] = total
 
 
-def finish(place, mine_ref, other_ref, core_sketch_ref, corange_ref, core_ref):
+def turn_out(place, part_ref, corange_ref):
     rank, slabs, _ = corange_ref.shape
+    for j in range(slabs):
+        corange_ref[:, j, :] = part_ref[SLAB * j : SLAB * j + rank, :]
+
+
+def finish(place, mine_ref, other_ref, core_sketch_ref, before, corange_ref, core_ref):
+    turn_out(place, other_ref, corange_ref)
     size = core_ref.shape[0]
     more = size - 256
     for own in range(2):
@@ -147,8 +153,6 @@
         def _():
             for half, part in ((own, mine_ref), (1 - own, other_ref)):
                 lanes = slice(128 * half, 128 * half + 128)
-                for j in range(slabs):
-                    corange_ref[:, j, lanes] = part[SLAB * j : SLAB * j + rank, :]
                 core_ref[:, lanes] = core_sketch_ref[:, lanes] + part[CORE_AT : CORE_AT + size, :]
                 block = jnp.concatenate([part[EXTRA_AT : EXTRA_AT + 8, :], jnp.zeros((120, 128), jnp.float32)], axis=0)
                 turned = block.T
@@ -257,15 +261,35 @@
         copies = add_up(sum_stack, "sum_stack", (16, CHUNK, 128), place, stack, keep)
         mine = lax.all_to_all(copies, ("x", "y"), 0, 0, tiled=True).reshape(ROWS, 128)
         other = lax.ppermute(mine, "core", swap)
+        whole = [pl.BlockSpec((ROWS, 128), lambda i, p: (0, 0))] * 2
+        core_spec = pl.BlockSpec((size, size), lambda i, p: (0, 0))
+        own_half = pl.pallas_call(
+            turn_out,
+            out_shape=f32(rank, slabs, cols),
+            grid_spec=pltpu.PrefetchScalarGridSpec(
+                num_scalar_prefetch=1,
+                grid=(1,),
+                in_specs=whole[:1],
+                out_specs=pl.BlockSpec((rank, slabs, 128), lambda i, p: (0, 0, p[1])),
+            ),
+            compiler_params=params,
+            cost_estimate=cost(1),
+            name="own_half",
+        )(place, mine)
         corange_out, core_out = pl.pallas_call(
             finish,
             out_shape=(f32(rank, slabs, cols), f32(size, size)),
-            in_specs=[smem] + [vmem] * 3,
-            out_specs=[vmem] * 2,
+            grid_spec=pltpu.PrefetchScalarGridSpec(
+                num_scalar_prefetch=1,
+                grid=(1,),
+                in_specs=whole + [core_spec, anywhere],
+                out_specs=[pl.BlockSpec((rank, slabs, 128), lambda i, p: (0, 0, 1 - p[1])), core_spec],
+            ),
+            input_output_aliases={4: 0},
             compiler_params=params,
             cost_estimate=cost(2),
             name="finish",
-        )(place, mine, other, core_sketch)
+        )(place, mine, other, core_sketch, own_half)
         return keep, corange_out, core_out
 
     def nothing(*_):

time: 79.5 us -> 79.5 us (level)
  waiting for transfers between devices: 6.92 us -> 5.54 us
  Pallas kernels: 24.2 us -> 25.4 us
    ppermute x1, waiting for transfers between devices: 1.44 us -> 0.05 us  [reduce(): other = lax.ppermute(mine, 'core', swap)]
    pallas_call x0 -> x1, Pallas kernels: none -> 1.39 us  [reduce(): pl.pallas_call(turn_out, out_shape=f32(rank, slabs, cols), grid_spec=pltp...]
  transfers between devices with their start and end apart: 4 -> 4, of which waited for: 3 -> 3; matrix products, arithmetic and copies ran while one was open for 1% -> 1% of each run, Pallas kernels for 24% -> 25%
where the time goes in v4:
time: 79.5 us; the launch traced here: 79.1 us
  blocking collectives  28.8 us (36%)
  Pallas kernels  25.4 us (32%)
  starting transfers between devices  16.6 us (21%)
  waiting for transfers between devices  5.54 us (7%)
  other arithmetic  2.02 us (3%)
    all_to_all x1, blocking collectives, reduce(): lax.all_to_all(part.reshape(16, CHUNK, 128), ('x', 'y'), 0, 0, tiled=True)  16.4 us
    all_to_all x1, blocking collectives, reduce(): lax.all_to_all(copies, ('x', 'y'), 0, 0, tiled=True).reshape(ROWS, 128)  12.4 us
    pallas_call x1, Pallas kernels, reduce(): pl.pallas_call(products, out_shape=(f32(ROWS, 128), f32(ROWS, 128)), grid...  10.9 us
    pallas_call x2, Pallas kernels, range_part(): pl.pallas_call(range_half, out_shape=f32(rank, width), in_specs=[smem, an...  10.2 us
    ppermute x1, starting transfers between devices, on_device(): got = lax.ppermute(send, 'zh', swap)  7.83 us
    ppermute x1, starting transfers between devices, reduce(): other = lax.ppermute(mine, 'core', swap)  4.32 us
    all_to_all x1, waiting for transfers between devices, reduce(): stack = lax.all_to_all(copies, ('zh', 'zl'), 0, 0, tiled=True)  3.83 us
    all_to_all x1, starting transfers between devices, reduce(): stack = lax.all_to_all(copies, ('zh', 'zl'), 0, 0, tiled=True)  3.4 us
  transfers between devices with their start and end apart: 4, of which 3 were waited for; matrix products, arithmetic and copies ran while one was open for 1% of the time, Pallas kernels for 25%

profile of v4, /device:TPU:1, one launch (start us, length us, event | category | flops | bytes accessed | tf_op | source)
XLA Modules:
  0.0 79.1 jit_solution(4249695053000868249)
XLA Ops:
  0.6 0.0 copy-start.2
  0.6 5.3 %range_send.1 = f32[129,1024]{1,0:T(8,128)} custom-call(s32[1]{0:T(128)} %bitcast.6.place, f32[4,2048,256]{2,1,0:T(8,128)} %snap_hbm.1, f32[129,4,256]{2,1,0:T(4,128)} %bitcast.14), custom_call_target="tpu_custom_call" | custom-call | flops 5000000000 | bytes 15000000 | tf_op jit(solution)/shard_map/range_send/pallas_call | solution.py:187
  5.9 7.8 %collective-permute-start.2 = (f32[129,1024]{1,0:T(8,128)}, f32[129,1024]{1,0:T(8,128)S(1)}, u32[]{:S(2)}, u32[]{:S(2)}) collective-permute-start(f32[129,1024]{1,0:T(8,128)} %range_send.1), channel_id=1, source_target_pairs={{0,1},{1,0},{2,3},{3,2},{4,5},{5,4},{6,7},{7,6},{8,9},{9,8},{10,11... | collective-permute-start | bytes 1585160 | tf_op jit(solution)/shard_map/ppermute | solution.py:219
  13.7 0.1 pad_add_fusion
  13.8 0.0 copy-done.2
  13.8 64.4 %conditional.1 = (f32[129,1024]{1,0:T(8,128)S(1)}, f32[129,4,256]{2,1,0:T(4,128)}, f32[259,259]{1,0:T(8,128)}) conditional(s32[]{:T(128)} %convert_element_type.3, () %tuple.16, (s32[3]{0:T(128)S(1)}, f32[4,2048,256]{2,1,0:T(8,128)}, f32[129,2048]{1,0:T(8,128)}, f32[259,2048]{1,0:T(8,128)S(1)}, f32[259,4,256]{2,1,0:T(4,128)}, ...), branch_computations={%region_0.0_spmd, %region_1.0_spmd} | conditional | flops 19000111104 | bytes 74097128 | solution.py:298
  13.8 10.9 %products.1 = (f32[896,128]{1,0:T(8,128)}, f32[896,128]{1,0:T(8,128)}) custom-call(s32[3]{0:T(128)S(1)} %get-tuple-element.18.place, f32[4,2048,256]{2,1,0:T(8,128)} %get-tuple-element.19.snap_ref.snap_hbm, f32[129,2048]{1,0:T(8,128)} %get-tuple-element.44.corange_ref, f32[259,2048]{1,0:T(8,128)S(1)} %get-tuple-element.45.left_ref, ...), custom_call_target="tpu_custom_call" | custom-call | flops 8999999488 | bytes 27000000 | tf_op jit(solution)/shard_map/cond/branch_1_fun/products/pallas_call | solution.py:224
  24.7 1.0 %collective-permute-start = (f32[896,128]{1,0:T(8,128)}, f32[896,128]{1,0:T(8,128)S(1)}, u32[]{:S(2)}, u32[]{:S(2)}) collective-permute-start(f32[896,128]{1,0:T(8,128)} %get-tuple-element.27), channel_id=1, source_target_pairs={{0,2},{2,0},{1,3},{3,1},{4,6},{6,4},{5,7},{7,5},{8,10},{10,8},{9,1... | collective-permute-start | bytes 1376264 | tf_op jit(solution)/shard_map/cond/branch_1_fun/ppermute | solution.py:256
  25.7 1.7 %collective-permute-done = f32[896,128]{1,0:T(8,128)S(1)} collective-permute-done((f32[896,128]{1,0:T(8,128)}, f32[896,128]{1,0:T(8,128)S(1)}, u32[]{:S(2)}, u32[]{:S(2)}) %collective-permute-start) | collective-permute-done | bytes 458784 | tf_op jit(solution)/shard_map/cond/branch_1_fun/ppermute | solution.py:256
  27.4 1.1 %add.6 = f32[896,128]{1,0:T(8,128)S(1)} add(f32[896,128]{1,0:T(8,128)} %get-tuple-element.26, f32[896,128]{1,0:T(8,128)S(1)} %collective-permute-done) | non-fusion elementwise | flops 114688 | bytes 1376256 | tf_op jit(solution)/shard_map/cond/branch_1_fun/add | solution.py:256
  28.4 16.4 %all_to_all.12.pieces_ref = f32[16,56,128]{2,1,0:T(8,128)S(1)} all-to-all(f32[16,56,128]{2,1,0:T(8,128)S(1)} %bitcast.12), channel_id=1, replica_groups=mesh['zl'=4,'x'=4,'y'=4,'core'=2,'zh'=2] {'x','y'}, dimensions={0} | all-to-all | bytes 917504 | tf_op jit(solution)/shard_map/cond/branch_1_fun/all_to_all | solution.py:257
  44.8 0.0 copy-start.3
  44.8 0.0 copy-start.4
  44.8 0.7 sum_pieces.1.rest_1_
  45.6 3.4 %all-to-all-start.1 = ((f32[8,56,128]{2,1,0:T(8,128)}), f32[8,56,128]{2,1,0:T(8,128)S(1)}, u32[]{:S(2)}, u32[]{:S(2)}) async-start(f32[8,56,128]{2,1,0:T(8,128)} %sum_pieces.1.rest_1_), calls=%async_computation.1 | async-start | bytes 458752 | tf_op jit(solution)/shard_map/cond/branch_1_fun/all_to_all | solution.py:259
  49.0 0.0 copy-done.3
  49.0 0.0 copy-done.4
  49.0 4.9 %range_keep.1.rest_0_ = f32[129,1024]{1,0:T(8,128)S(1)} custom-call(s32[3]{0:T(128)S(1)} %get-tuple-element.18.place, f32[4,2048,256]{2,1,0:T(8,128)} %get-tuple-element.19.snap_ref.snap_hbm, f32[129,4,256]{2,1,0:T(4,128)S(1)} %copy-done.4, f32[129,1024]{1,0:T(8,128)S(1)} %copy-done.3, f32[8,56,128]{2,1,0:T(8,128)} %sum_pieces.1.rest_1_), custom_call_target="tpu_custom_call" | custom-call | flops 5000000000 | bytes 15000000 | tf_op jit(solution)/shard_map/cond/branch_1_fun/range_keep/pallas_call | solution.py:187
  53.9 0.0 copy-start
  53.9 3.8 %all-to-all-done.1.stack_ref = f32[8,56,128]{2,1,0:T(8,128)S(1)} async-done(((f32[8,56,128]{2,1,0:T(8,128)}), f32[8,56,128]{2,1,0:T(8,128)S(1)}, u32[]{:S(2)}, u32[]{:S(2)}) %all-to-all-start.1) | async-done | bytes 229408 | tf_op jit(solution)/shard_map/cond/branch_1_fun/all_to_all | solution.py:259
  57.8 0.6 sum_stack.1
  58.4 0.0 copy-start.5
  58.4 12.4 %all_to_all.13 = f32[16,56,128]{2,1,0:T(8,128)S(1)} all-to-all(f32[16,56,128]{2,1,0:T(8,128)S(1)} %sum_stack.1), channel_id=1, replica_groups=mesh['zl'=4,'x'=4,'y'=4,'core'=2,'zh'=2] {'x','y'}, dimensions={0} | all-to-all | bytes 917504 | tf_op jit(solution)/shard_map/cond/branch_1_fun/all_to_all | solution.py:262
  70.8 0.0 copy-done
  70.8 4.3 %collective-permute-start.1 = (f32[896,128]{1,0:T(8,128)S(1)}, f32[896,128]{1,0:T(8,128)S(1)}, u32[]{:S(2)}, u32[]{:S(2)}) collective-permute-start(f32[896,128]{1,0:T(8,128)S(1)} %bitcast.9), channel_id=1, source_target_pairs={{0,2},{2,0},{1,3},{3,1},{4,6},{6,4},{5,7},{7,5},{8,10},{10,8},{9,1... | collective-permute-start | bytes 1376264 | tf_op jit(solution)/shard_map/cond/branch_1_fun/ppermute | solution.py:263
  75.1 1.4 %own_half.1.before = f32[129,4,256]{2,1,0:T(4,128)} custom-call(s32[3]{0:T(128)S(1)} %get-tuple-element.18.place, f32[896,128]{1,0:T(8,128)S(1)} %bitcast.10), custom_call_target="tpu_custom_call" | custom-call | flops 1000000000 | bytes 3000000 | tf_op jit(solution)/shard_map/cond/branch_1_fun/own_half/pallas_call | solution.py:266
  76.5 0.1 collective-permute-done.1.other_ref
  76.6 0.0 copy-done.5
  76.6 1.7 %finish.1 = (f32[129,4,256]{2,1,0:T(4,128)}, f32[259,259]{1,0:T(8,128)}) custom-call(s32[3]{0:T(128)S(1)} %get-tuple-element.18.place, f32[896,128]{1,0:T(8,128)S(1)} %bitcast.11, f32[896,128]{1,0:T(8,128)S(1)} %collective-permute-done.1.other_ref, f32[259,259]{1,0:T(8,128)S(1)} %copy-done.5, ...), custom_call_target="tpu_custom_call", output_to_operand_aliasing={{0}: (4, {})} | custom-call | flops 2000000000 | bytes 6000000 | tf_op jit(solution)/shard_map/cond/branch_1_fun/finish/pallas_call | solution.py:279
  78.2 0.0 copy-done.1
  78.2 0.0 collective-permute-done.2
  78.2 0.9 %add.10 = f32[129,1024]{1,0:T(8,128)} add(f32[129,1024]{1,0:T(8,128)S(1)} %get-tuple-element.37, f32[129,1024]{1,0:T(8,128)S(1)} %collective-permute-done.2) | non-fusion elementwise | flops 132096 | bytes 1585152 | tf_op jit(solution)/shard_map/add | solution.py:302
  (1 shorter events, 0.0 us)
Async XLA Ops:
  0.6 13.2 %copy-start.2 = (f32[259,2048]{1,0:T(8,128)S(1)}, f32[259,2048]{1,0:T(8,128)}, u32[]{:S(2)}) copy-start(f32[259,2048]{1,0:T(8,128)} %param.12) | copy-start | bytes 6365188
  5.9 72.3 %collective-permute-start.2 = (f32[129,1024]{1,0:T(8,128)}, f32[129,1024]{1,0:T(8,128)S(1)}, u32[]{:S(2)}, u32[]{:S(2)}) collective-permute-start(f32[129,1024]{1,0:T(8,128)} %range_send.1), channel_id=1, source_target_pairs={{0,1},{1,0},{2,3},{3,2},{4,5},{5,4},{6,7},{7,6},{8,9},{9,8},{10,11... | collective-permute-start | bytes 1585160 | tf_op jit(solution)/shard_map/ppermute | solution.py:219
  24.7 2.7 %collective-permute-start = (f32[896,128]{1,0:T(8,128)}, f32[896,128]{1,0:T(8,128)S(1)}, u32[]{:S(2)}, u32[]{:S(2)}) collective-permute-start(f32[896,128]{1,0:T(8,128)} %get-tuple-element.27), channel_id=1, source_target_pairs={{0,2},{2,0},{1,3},{3,1},{4,6},{6,4},{5,7},{7,5},{8,10},{10,8},{9,1... | collective-permute-start | bytes 1376264 | tf_op jit(solution)/shard_map/cond/branch_1_fun/ppermute | solution.py:256
  44.8 4.1 %copy-start.3 = (f32[129,1024]{1,0:T(8,128)S(1)}, f32[129,1024]{1,0:T(8,128)}, u32[]{:S(2)}) copy-start(f32[129,1024]{1,0:T(8,128)} %get-tuple-element.46.rest_0_) | copy-start | bytes 1585156 | tf_op jit(solution)/shard_map/cond
  44.8 4.1 %copy-start.4 = (f32[129,4,256]{2,1,0:T(4,128)S(1)}, f32[129,4,256]{2,1,0:T(4,128)}, u32[]{:S(2)}) copy-start(f32[129,4,256]{2,1,0:T(4,128)} %get-tuple-element.20.test_hbm) | copy-start | bytes 1585156 | tf_op jit(solution)/shard_map/cond
  45.6 12.2 %all-to-all-start.1 = ((f32[8,56,128]{2,1,0:T(8,128)}), f32[8,56,128]{2,1,0:T(8,128)S(1)}, u32[]{:S(2)}, u32[]{:S(2)}) async-start(f32[8,56,128]{2,1,0:T(8,128)} %sum_pieces.1.rest_1_), calls=%async_computation.1 | async-start | bytes 458752 | tf_op jit(solution)/shard_map/cond/branch_1_fun/all_to_all | solution.py:259
  53.9 16.9 %copy-start = (f32[129,1024]{1,0:T(8,128)}, f32[129,1024]{1,0:T(8,128)S(1)}, u32[]{:S(2)}) copy-start(f32[129,1024]{1,0:T(8,128)S(1)} %range_keep.1.rest_0_) | copy-start | bytes 1585156 | tf_op jit(solution)/shard_map/cond
  58.4 18.2 %copy-start.5 = (f32[259,259]{1,0:T(8,128)S(1)}, f32[259,259]{1,0:T(8,128)}, u32[]{:S(2)}) copy-start(f32[259,259]{1,0:T(8,128)} %get-tuple-element.47.core_sketch_ref) | copy-start | bytes 804976 | tf_op jit(solution)/shard_map/cond
  70.8 5.8 %collective-permute-start.1 = (f32[896,128]{1,0:T(8,128)S(1)}, f32[896,128]{1,0:T(8,128)S(1)}, u32[]{:S(2)}, u32[]{:S(2)}) collective-permute-start(f32[896,128]{1,0:T(8,128)S(1)} %bitcast.9), channel_id=1, source_target_pairs={{0,2},{2,0},{1,3},{3,1},{4,6},{6,4},{5,7},{7,5},{8,10},{10,8},{9,1... | collective-permute-start | bytes 1376264 | tf_op jit(solution)/shard_map/cond/branch_1_fun/ppermute | solution.py:263
  76.6 1.7 %copy-start.1 = (f32[129,1024]{1,0:T(8,128)S(1)}, f32[129,1024]{1,0:T(8,128)}, u32[]{:S(2)}) copy-start(f32[129,1024]{1,0:T(8,128)} %copy-done) | copy-start | bytes 1585156 | tf_op jit(solution)/shard_map/cond
